TPU v7x, 256 devices: a whole 4x4x8 slice. The times are simulated.
256 devices in a mesh: fsdp: 64 (over z, x, core), tensor: 4 (over y).
Axes of the slice: x: 4, y: 4, z: 8, core: 2. Of those that a mesh axis runs over, the one named last changes fastest.
Arguments:
- grad: bfloat16 [26624, 8192], P('fsdp', 'tensor'), may hold values from -6 to 6
- momentum: float32 [26624, 8192], P('fsdp', 'tensor'), may hold values from -6 to 6
- basis: bfloat16 [8192, 256], P('tensor'), may hold values from -0.0625 to 0.0625
Outputs:
- new_momentum: float32 [26624, 8192], P('fsdp', 'tensor')
- update: bfloat16 [26624, 8192], P('fsdp', 'tensor')
- basis_next: bfloat16 [8192, 256], P('tensor')
All inputs are finite; a program needn't handle non-finite values.
Results may differ from a plain program's by a relative error of at most 0.0058.
Values may be sent and summed in bfloat16 or wider, within the bound.
A program may use at most 64 MiB of HBM per device.

v0:
```python
import math

import jax
import jax.numpy as jnp
from jax import lax
from jax.sharding import PartitionSpec as P


def partner_2(block, axis, apart):
    count = lax.axis_size(axis)
    route = []
    for low in range(count):
        high = low | 1 << apart
        if high != low and high < count:
            route += [(low, high), (high, low)]
    return lax.ppermute(block, axis, route)


def upper_factor(gram):
    return jnp.linalg.cholesky(gram).T


def on_device(grad, momentum, basis):
    high = lax.Precision.HIGHEST
    rows_here = grad.shape[0]
    cols_here = grad.shape[1]
    rank_cols = basis.shape[1]
    blended = momentum + grad.astype(jnp.float32)
    partial_panel = jnp.dot(blended, basis.astype(jnp.float32), precision=high)
    panel = lax.psum(partial_panel, "tensor")
    gram_local = jnp.dot(panel.T, panel, precision=high)
    tri = upper_factor(gram_local)
    my_index = lax.axis_index("fsdp")
    levels = lax.axis_size("fsdp").bit_length() - 1
    for level in range(levels):
        partner = partner_2(tri, "fsdp", level)
        is_lower = my_index >> level & 1 == 0
        first = jnp.where(is_lower, tri, partner)
        second = jnp.where(is_lower, partner, tri)
        merged = jnp.dot(first.T, first, precision=high) + jnp.dot(second.T, second, precision=high)
        tri = upper_factor(merged)
    ortho = jax.scipy.linalg.solve_triangular(tri.T, panel.T, lower=True).T
    partial_proj = lax.dot_general(blended, ortho, (((0,), (0,)), ((), ())), precision=high)
    projected = lax.psum(partial_proj, "fsdp")
    rounded = lax.optimization_barrier(projected.astype(jnp.bfloat16))
    rounded_f = rounded.astype(jnp.float32)
    new_momentum = blended - 0.05 * jnp.dot(ortho, rounded_f.T, precision=high)
    column_sq = lax.psum(jnp.sum(rounded_f * rounded_f, axis=0), "tensor")
    basis_next = lax.optimization_barrier(
        (rounded_f * lax.rsqrt(column_sq + 1e-06)[None, :]).astype(jnp.bfloat16)
    )
    total_rows = rows_here * lax.axis_size("fsdp")
    total_cols = cols_here * lax.axis_size("tensor")
    factor = math.sqrt(total_rows * total_cols / rank_cols)
    update = (factor * jnp.dot(ortho, basis_next.astype(jnp.float32).T, precision=high)).astype(
        jnp.bfloat16
    )
    return (new_momentum, update, basis_next)


def solution(mesh):
    return jax.shard_map(
        on_device,
        mesh=mesh,
        in_specs=(P("fsdp", "tensor"), P("fsdp", "tensor"), P("tensor", None)),
        out_specs=(P("fsdp", "tensor"), P("fsdp", "tensor"), P("tensor", None)),
        check_vma=False,
    )
```

profile of v0, /device:TPU:1, one launch (start us, length us, event | category | flops | bytes accessed | tf_op | source)
XLA Modules:
  0.0 725.7 jit_solution(15754139986557807254)
XLA Ops:
  13.5 49.5 %all-reduce.4.cloned.1.call-done = f32[416,256]{1,0:T(8,128)} async-done(((f32[416,256]{1,0:T(8,128)}), f32[416,256]{1,0:T(8,128)}) %all-reduce.4.cloned.1.call-update) | async-done | bytes 426000 | tf_op jit(solution)/shard_map/psum | solution.py:30
  65.3 11.7 %cholesky.340 = f32[128,128]{1,0:T(8,128)S(1)} custom-call(f32[128,128]{1,0:T(8,128)S(1)} %cholesky.574), custom_call_target="Cholesky" | custom-call | tf_op jit(solution)/shard_map/jit(cholesky)/cholesky | solution.py:20
  77.0 9.8 %custom-call.19 = f32[1,128,128]{1,2,0:T(8,128)S(1)} custom-call(f32[1,128,128]{2,1,0:T(8,128)S(1)} %get-tuple-element.49), custom_call_target="InvertDiagBlocksLowerTriangular" | custom-call | tf_op jit(solution)/shard_map/jit(cholesky)/cholesky | solution.py:20
  87.3 12.2 %cholesky.357 = f32[128,128]{1,0:T(8,128)S(1)} custom-call(f32[128,128]{1,0:T(8,128)S(1)} %convolution_subtract_fusion.7), custom_call_target="Cholesky" | custom-call | tf_op jit(solution)/shard_map/jit(cholesky)/cholesky | solution.py:20
  106.4 11.7 %cholesky.374 = f32[128,128]{1,0:T(8,128)S(1)} custom-call(f32[128,128]{1,0:T(8,128)S(1)} %cholesky.577), custom_call_target="Cholesky" | custom-call | tf_op jit(solution)/shard_map/jit(cholesky)/cholesky | solution.py:20
  118.2 9.8 %custom-call.20 = f32[1,128,128]{1,2,0:T(8,128)S(1)} custom-call(f32[1,128,128]{2,1,0:T(8,128)S(1)} %get-tuple-element.45), custom_call_target="InvertDiagBlocksLowerTriangular" | custom-call | tf_op jit(solution)/shard_map/jit(cholesky)/cholesky | solution.py:20
  128.5 11.7 %cholesky.391 = f32[128,128]{1,0:T(8,128)S(1)} custom-call(f32[128,128]{1,0:T(8,128)S(1)} %convolution_subtract_fusion.6), custom_call_target="Cholesky" | custom-call | tf_op jit(solution)/shard_map/jit(cholesky)/cholesky | solution.py:20
  151.7 11.7 %cholesky.408 = f32[128,128]{1,0:T(8,128)S(1)} custom-call(f32[128,128]{1,0:T(8,128)S(1)} %cholesky.580), custom_call_target="Cholesky" | custom-call | tf_op jit(solution)/shard_map/jit(cholesky)/cholesky | solution.py:20
  163.5 9.8 %custom-call.21 = f32[1,128,128]{1,2,0:T(8,128)S(1)} custom-call(f32[1,128,128]{2,1,0:T(8,128)S(1)} %get-tuple-element.41), custom_call_target="InvertDiagBlocksLowerTriangular" | custom-call | tf_op jit(solution)/shard_map/jit(cholesky)/cholesky | solution.py:20
  173.8 11.7 %cholesky.425 = f32[128,128]{1,0:T(8,128)S(1)} custom-call(f32[128,128]{1,0:T(8,128)S(1)} %convolution_subtract_fusion.5), custom_call_target="Cholesky" | custom-call | tf_op jit(solution)/shard_map/jit(cholesky)/cholesky | solution.py:20
  197.6 11.7 %cholesky.442 = f32[128,128]{1,0:T(8,128)S(1)} custom-call(f32[128,128]{1,0:T(8,128)S(1)} %cholesky.583), custom_call_target="Cholesky" | custom-call | tf_op jit(solution)/shard_map/jit(cholesky)/cholesky | solution.py:20
  209.4 9.8 %custom-call.22 = f32[1,128,128]{1,2,0:T(8,128)S(1)} custom-call(f32[1,128,128]{2,1,0:T(8,128)S(1)} %get-tuple-element.37), custom_call_target="InvertDiagBlocksLowerTriangular" | custom-call | tf_op jit(solution)/shard_map/jit(cholesky)/cholesky | solution.py:20
  219.6 11.7 %cholesky.459 = f32[128,128]{1,0:T(8,128)S(1)} custom-call(f32[128,128]{1,0:T(8,128)S(1)} %convolution_subtract_fusion.4), custom_call_target="Cholesky" | custom-call | tf_op jit(solution)/shard_map/jit(cholesky)/cholesky | solution.py:20
  241.2 11.7 %cholesky.476 = f32[128,128]{1,0:T(8,128)S(1)} custom-call(f32[128,128]{1,0:T(8,128)S(1)} %cholesky.586), custom_call_target="Cholesky" | custom-call | tf_op jit(solution)/shard_map/jit(cholesky)/cholesky | solution.py:20
  253.0 9.8 %custom-call.23 = f32[1,128,128]{1,2,0:T(8,128)S(1)} custom-call(f32[1,128,128]{2,1,0:T(8,128)S(1)} %get-tuple-element.33), custom_call_target="InvertDiagBlocksLowerTriangular" | custom-call | tf_op jit(solution)/shard_map/jit(cholesky)/cholesky | solution.py:20
  263.3 11.7 %cholesky.493 = f32[128,128]{1,0:T(8,128)S(1)} custom-call(f32[128,128]{1,0:T(8,128)S(1)} %convolution_subtract_fusion.3), custom_call_target="Cholesky" | custom-call | tf_op jit(solution)/shard_map/jit(cholesky)/cholesky | solution.py:20
  280.1 11.4 %collective-permute-done.4 = f32[256,256]{0,1:T(8,128)S(1)} collective-permute-done((f32[256,256]{0,1:T(8,128)S(1)}, f32[256,256]{0,1:T(8,128)S(1)}, u32[]{:S(2)}, u32[]{:S(2)}) %collective-permute-start.4) | collective-permute-done | bytes 262176 | tf_op jit(solution)/shard_map/ppermute | solution.py:16
  292.6 11.7 %cholesky.510 = f32[128,128]{1,0:T(8,128)S(1)} custom-call(f32[128,128]{1,0:T(8,128)S(1)} %cholesky.589), custom_call_target="Cholesky" | custom-call | tf_op jit(solution)/shard_map/jit(cholesky)/cholesky | solution.py:20
  314.7 11.7 %cholesky.527 = f32[128,128]{1,0:T(8,128)S(1)} custom-call(f32[128,128]{1,0:T(8,128)S(1)} %convolution_subtract_fusion.2), custom_call_target="Cholesky" | custom-call | tf_op jit(solution)/shard_map/jit(cholesky)/cholesky | solution.py:20
  350.3 11.7 %cholesky.544 = f32[128,128]{1,0:T(8,128)S(1)} custom-call(f32[128,128]{1,0:T(8,128)S(1)} %cholesky.592), custom_call_target="Cholesky" | custom-call | tf_op jit(solution)/shard_map/jit(cholesky)/cholesky | solution.py:20
  375.4 11.7 %cholesky.561 = f32[128,128]{1,0:T(8,128)S(1)} custom-call(f32[128,128]{1,0:T(8,128)S(1)} %convolution_subtract_fusion.1), custom_call_target="Cholesky" | custom-call | tf_op jit(solution)/shard_map/jit(cholesky)/cholesky | solution.py:20
  398.9 20.5 %custom-call.12 = f32[2,128,128]{1,2,0:T(8,128)S(1)} custom-call(f32[2,128,128]{2,1,0:T(8,128)} %copy-done.7), custom_call_target="InvertDiagBlocksLowerTriangular" | custom-call | tf_op jit(solution)/shard_map/jit(_solve_triangular)/triangular_solve | solution.py:42
  421.2 10.0 %fusion.2 = f32[2048,256]{1,0:T(8,128)} fusion(f32[416,2048]{1,0:T(8,128)} %param.5, bf16[416,2048]{1,0:T(8,128)(2,1)S(1)} %copy-done.1, f32[128,416]{0,1:T(8,128)S(1)} %fusion.44, f32[128,416]{0,1:T(8,128)S(1)} %fusion.29), kind=kOutput, calls=%fused_computation.9 | convolution fusion | flops 2619056128 | bytes 7634944 | tf_op jit(solution)/shard_map/dot_general | solution.py:43
  431.2 270.7 %all-reduce.5 = bf16[2048,256]{1,0:T(8,128)(2,1)S(1)} all-reduce(f32[2048,256]{1,0:T(8,128)} %fusion.2), channel_id=1, replica_groups=mesh['fsdp'=64,'tensor'=4] {'fsdp'}, use_global_device_ids=true, to_apply=%region_5.7 | all-reduce | flops 524288 | bytes 3145728 | tf_op jit(solution)/shard_map/psum | solution.py:44
  (140 shorter events, 132.0 us)
Async XLA Ops:
  7.2 1.2 copy-start
  7.2 55.7 %all-reduce.4.cloned.1.call-start = ((), (), s32[]{:S(2)}) async-start(), calls=%async_computation | async-start | bytes 851968 | tf_op jit(solution)/shard_map/psum | solution.py:30
  101.5 3.9 collective-permute-start
  142.9 7.8 %collective-permute-start.1 = (f32[256,256]{0,1:T(8,128)S(1)}, f32[256,256]{0,1:T(8,128)S(1)}, u32[]{:S(2)}, u32[]{:S(2)}) collective-permute-start(f32[256,256]{0,1:T(8,128)S(1)} %select_bitcast_fusion.4), channel_id=1, source_target_pairs={{0,8},{8,0},{4,12},{12,4},{16,24},{24,16},{20,28},{28,20},{32,40},... | collective-permute-start | bytes 786440 | tf_op jit(solution)/shard_map/ppermute | solution.py:16
  188.1 8.4 %collective-permute-start.2 = (f32[256,256]{0,1:T(8,128)S(1)}, f32[256,256]{0,1:T(8,128)S(1)}, u32[]{:S(2)}, u32[]{:S(2)}) collective-permute-start(f32[256,256]{0,1:T(8,128)S(1)} %select_bitcast_fusion.3), channel_id=1, source_target_pairs={{0,16},{16,0},{4,20},{20,4},{8,24},{24,8},{12,28},{28,12},{32,48},... | collective-permute-start | bytes 786440 | tf_op jit(solution)/shard_map/ppermute | solution.py:16
  234.0 6.2 collective-permute-start.3
  277.6 13.9 %collective-permute-start.4 = (f32[256,256]{0,1:T(8,128)S(1)}, f32[256,256]{0,1:T(8,128)S(1)}, u32[]{:S(2)}, u32[]{:S(2)}) collective-permute-start(f32[256,256]{0,1:T(8,128)S(1)} %select_bitcast_fusion.1), channel_id=1, source_target_pairs={{0,64},{64,0},{4,68},{68,4},{8,72},{72,8},{12,76},{76,12},{16,80},... | collective-permute-start | bytes 786440 | tf_op jit(solution)/shard_map/ppermute | solution.py:16
  314.4 104.9 %copy-start.3 = (f32[416,256]{1,0:T(8,128)S(1)}, f32[416,256]{1,0:T(8,128)}, u32[]{:S(2)}) copy-start(f32[416,256]{1,0:T(8,128)} %all-reduce.4.cloned.1.call-done) | copy-start | bytes 1277956
  329.0 14.3 %copy-start.4 = (f32[256,256]{0,1:T(8,128)}, f32[256,256]{0,1:T(8,128)S(1)}, u32[]{:S(2)}) copy-start(f32[256,256]{0,1:T(8,128)S(1)} %select_bitcast_fusion) | copy-start | bytes 786436
  329.1 14.3 %collective-permute-start.5 = (f32[256,256]{0,1:T(8,128)S(1)}, f32[256,256]{0,1:T(8,128)S(1)}, u32[]{:S(2)}, u32[]{:S(2)}) collective-permute-start(f32[256,256]{0,1:T(8,128)S(1)} %select_bitcast_fusion), channel_id=1, source_target_pairs={{0,128},{128,0},{4,132},{132,4},{8,136},{136,8},{12,140},{140,12},... | collective-permute-start | bytes 786440 | tf_op jit(solution)/shard_map/ppermute | solution.py:16
  343.3 0.7 copy-start.5
  344.4 76.8 %copy-start.1 = (bf16[416,2048]{1,0:T(8,128)(2,1)S(1)}, bf16[416,2048]{1,0:T(8,128)(2,1)}, u32[]{:S(2)}) copy-start(bf16[416,2048]{1,0:T(8,128)(2,1)} %param.4) | copy-start | bytes 5111812
  349.6 0.7 copy-start.6
  398.2 0.7 copy-start.7
  715.9 2.8 copy-start.2
Sparse Core Ops, SparseCore 0:
  13.6 49.2 all-reduce.3
where the time goes:
time: 740 us; the launch traced here: 726 us
  blocking collectives  278 us (38%)
  other arithmetic  267 us (36%)
  waiting for transfers between devices  86.3 us (12%)
  matrix products  40.3 us (5%)
  between operations  23.9 us (3%)
  starting transfers between devices  17.6 us (2%)
  local copies, waits for them, and re-layouts  12.5 us (2%)
    psum x1, blocking collectives, on_device(): projected = lax.psum(partial_proj, 'fsdp')  271 us
    another operation x48, other arithmetic, upper_factor(): return jnp.linalg.cholesky(gram).T  242 us
    psum x1, waiting for transfers between devices, on_device(): panel = lax.psum(partial_panel, 'tensor')  49.5 us
    ppermute x6, waiting for transfers between devices, partner_2(): return lax.ppermute(block, axis, route)  36.8 us
    another operation x3, other arithmetic, on_device(): ortho = jax.scipy.linalg.solve_triangular(tri.T, panel.T, lower=True).T  22.2 us
    ppermute x6, starting transfers between devices, partner_2(): return lax.ppermute(block, axis, route)  17.6 us
  transfers between devices with their start and end apart: 7, of which 7 were waited for; matrix products, arithmetic and copies ran while one was open for 0% of the time, Pallas kernels for 0%

commit v1 on v0

v1 whole, which is shorter than its diff:
```python
import math

import jax
import jax.numpy as jnp
from jax import lax
from jax.experimental import pallas as pl
from jax.experimental.pallas import tpu as pltpu
from jax.sharding import PartitionSpec as P

HIGH = lax.Precision.HIGHEST
F32 = jnp.float32


def dot(a, b, dims):
    return lax.dot_general(a, b, (dims, ((), ())), precision=HIGH, preferred_element_type=F32)


def inverse_factor(square):
    size = square.shape[0]
    tall = size // 8
    tiles = [square[8 * i : 8 * i + 8, :] for i in range(tall)]
    lane = lax.broadcasted_iota(jnp.int32, (8, size), 1)
    sub = lax.broadcasted_iota(jnp.int32, (8, size), 0)
    pivots = []
    for t in range(tall):
        start = 8 * t
        left = tall - t
        cols = [
            [jnp.broadcast_to(tiles[i][:, start + l : start + l + 1], (8, size)) for i in range(t, tall)]
            for l in range(8)
        ]
        mult = [[None] * left for _ in range(8)]
        group = tiles[t]
        rows = []
        pivot = jnp.zeros((8, size), F32)
        for l in range(8):
            here = cols[l][0][l : l + 1, :]
            recip = jnp.broadcast_to(1.0 / here, (8, size))
            pivot = jnp.where(sub == l, here, pivot)
            mult[l][0] = jnp.where(sub > l, cols[l][0] * recip, 0.0)
            for i in range(1, left):
                mult[l][i] = cols[l][i] * recip
            for later in range(l + 1, 8):
                across = jnp.broadcast_to(cols[later][0][l : l + 1, :], (8, size))
                for i in range(left):
                    cols[later][i] = cols[later][i] - mult[l][i] * across
            at = start + l
            row = jnp.where(lane[:1] == at, 1.0, group[l : l + 1, :])
            group = jnp.where((lane == at) & (sub > l), 0.0, group)
            group = group - mult[l][0] * jnp.broadcast_to(row, (8, size))
            row = jnp.where((lane[:1] > at) & (lane[:1] < start + 8), 0.0, row)
            rows.append(jnp.broadcast_to(row, (8, size)))
        tiles[t] = group
        pivots.append(pivot)
        for i in range(1, left):
            total = mult[0][i] * rows[0]
            for l in range(1, 8):
                total = total + mult[l][i] * rows[l]
            kept = jnp.where((lane >= start) & (lane < start + 8), 0.0, tiles[t + i])
            tiles[t + i] = kept - total
    out = []
    for i in range(tall):
        at = sub + 8 * i
        unit = jnp.where(lane == at, 1.0, jnp.where(lane < at, tiles[i], 0.0))
        out.append(unit * lax.rsqrt(pivots[i]))
    return jnp.concatenate(out, 0)


def factor_kernel(gram_ref, out_ref):
    half = gram_ref.shape[0] // 2
    first = inverse_factor(gram_ref[:half, :half])
    across = dot(first, gram_ref[:half, half:], ((1,), (0,)))
    second = inverse_factor(gram_ref[half:, half:] - dot(across, across, ((0,), (0,))))
    below = -dot(across, first, ((0,), (0,)))
    out_ref[:half, :half] = first
    out_ref[:half, half:] = jnp.zeros((half, half), F32)
    out_ref[half:, :half] = dot(second, below, ((1,), (0,)))
    out_ref[half:, half:] = second


def factor(gram):
    return pl.pallas_call(
        factor_kernel,
        out_shape=jax.ShapeDtypeStruct(gram.shape, F32),
        in_specs=[pl.BlockSpec(memory_space=pltpu.VMEM)],
        out_specs=pl.BlockSpec(memory_space=pltpu.VMEM),
        compiler_params=pltpu.CompilerParams(vmem_limit_bytes=32 << 20),
    )(gram)


def on_device(grad, momentum, basis):
    rows_here, cols_here = grad.shape
    rank = basis.shape[1]
    blended = momentum + grad.astype(F32)
    panel = lax.psum(dot(blended, basis.astype(F32), ((1,), (0,))), "tensor")
    gram = lax.psum(dot(panel, panel, ((0,), (0,))), "fsdp")
    partial = dot(blended, panel, ((0,), (0,)))
    mine = lax.psum_scatter(partial, "fsdp", scatter_dimension=0, tiled=True)
    inverse = factor(gram)
    ortho = dot(panel, inverse, ((1,), (1,)))
    shard = dot(mine, inverse, ((1,), (1,))).astype(jnp.bfloat16)
    rounded = lax.all_gather(shard, "fsdp", axis=0, tiled=True)
    rounded_f = rounded.astype(F32)
    column_sq = lax.psum(jnp.sum(rounded_f * rounded_f, axis=0), "tensor")
    basis_next = (rounded_f * lax.rsqrt(column_sq + 1e-06)[None, :]).astype(jnp.bfloat16)
    ortho_b = ortho.astype(jnp.bfloat16)
    back = lax.dot_general(ortho_b, rounded, (((1,), (1,)), ((), ())), preferred_element_type=F32)
    new_momentum = blended - 0.05 * back
    scale = math.sqrt(rows_here * lax.axis_size("fsdp") * cols_here * lax.axis_size("tensor") / rank)
    step = lax.dot_general(ortho_b, basis_next, (((1,), (1,)), ((), ())), preferred_element_type=F32)
    update = (scale * step).astype(jnp.bfloat16)
    return (new_momentum, update, basis_next)


def solution(mesh):
    return jax.shard_map(
        on_device,
        mesh=mesh,
        in_specs=(P("fsdp", "tensor"), P("fsdp", "tensor"), P("tensor", None)),
        out_specs=(P("fsdp", "tensor"), P("fsdp", "tensor"), P("tensor", None)),
        check_vma=False,
    )
```

time: 740 us -> 491 us (0.66); the launches traced: 726 us -> 490 us
  waiting for transfers between devices: 86.3 us -> 427 us
  blocking collectives: 278 us -> 8.45 us
  other arithmetic: 267 us -> 3.11 us
  starting transfers between devices: 17.6 us -> 0.34 us
  matrix products: 40.3 us -> 26.6 us
  local copies, waits for them, and re-layouts: 12.5 us -> 2.14 us
  between operations: 23.9 us -> 13.8 us
  Pallas kernels: 0 us -> 8.56 us
    psum x1 -> x0, blocking collectives: 271 us -> none  [on_device(): projected = lax.psum(partial_proj, 'fsdp')]
    another operation x51 -> x0, other arithmetic: 265 us -> none  [the longest x48 242 us: upper_factor(): return jnp.linalg.cholesky(gram).T]
    psum x1 -> x2, waiting for transfers between devices: 49.5 us -> 219 us  [the longest x1 169 us: on_device(): gram = lax.psum(dot(panel, panel, ((0,), (0,))), 'fsdp')]
    reduce_scatter x0 -> x1, waiting for transfers between devices: none -> 128 us  [on_device(): mine = lax.psum_scatter(partial, 'fsdp', scatter_dimension=0, tiled=True)]
    all_gather x0 -> x1, waiting for transfers between devices: none -> 80.8 us  [on_device(): rounded = lax.all_gather(shard, 'fsdp', axis=0, tiled=True)]
    ppermute x6 -> x0, waiting for transfers between devices: 36.8 us -> none  [partner_2(): return lax.ppermute(block, axis, route)]
    ppermute x6 -> x0, starting transfers between devices: 17.6 us -> none  [partner_2(): return lax.ppermute(block, axis, route)]
    pallas_call x0 -> x1, Pallas kernels: none -> 8.56 us  [factor(): pl.pallas_call(factor_kernel, out_shape=jax.ShapeDtypeStruct(gram.shape,...]
  transfers between devices with their start and end apart: 7 -> 4, of which waited for: 7 -> 4; matrix products, arithmetic and copies ran while one was open for 0% -> 2% of each run, Pallas kernels for 0% -> 2%
where the time goes in v1:
time: 491 us; the launch traced here: 490 us
  waiting for transfers between devices  427 us (87%)
  matrix products  26.6 us (5%)
  between operations  13.8 us (3%)
  Pallas kernels  8.56 us (2%)
  blocking collectives  8.45 us (2%)
    psum x1, waiting for transfers between devices, on_device(): gram = lax.psum(dot(panel, panel, ((0,), (0,))), 'fsdp')  169 us
    reduce_scatter x1, waiting for transfers between devices, on_device(): mine = lax.psum_scatter(partial, 'fsdp', scatter_dimension=0, tiled=True)  128 us
    all_gather x1, waiting for transfers between devices, on_device(): rounded = lax.all_gather(shard, 'fsdp', axis=0, tiled=True)  80.8 us
    psum x1, waiting for transfers between devices, on_device(): panel = lax.psum(dot(blended, basis.astype(F32), ((1,), (0,))), 'tensor')  49.4 us
    dot_general x5, matrix products, dot(): lax.dot_general(a, b, (dims, ((), ())), precision=HIGH, preferred_element...  20.9 us
  transfers between devices with their start and end apart: 4, of which 4 were waited for; matrix products, arithmetic and copies ran while one was open for 2% of the time, Pallas kernels for 2%

profile of v1, /device:TPU:1, one launch (start us, length us, event | category | flops | bytes accessed | tf_op | source)
XLA Modules:
  0.0 490.4 jit_solution(4844896526721216035)
XLA Ops:
  7.2 0.0 all-reduce.3.cloned.1.call-start
  7.2 1.2 copy-done
  8.4 5.0 %fusion.3 = f32[416,256]{1,0:T(8,128)} fusion(bf16[2048,256]{1,0:T(8,128)(2,1)S(1)} %copy-done, f32[416,2048]{1,0:T(8,128)} %param.4, bf16[416,2048]{1,0:T(8,128)(2,1)} %param.3), kind=kOutput, calls=%fused_computation.8 | convolution fusion | flops 2618949632 | bytes 6586368 | tf_op jit(solution)/shard_map/dot_general | solution.py:15
  13.4 0.0 all-reduce.3.cloned.1.call-update
  13.5 0.0 all-reduce.5.cloned.1.call-start
  13.5 49.4 %all-reduce.3.cloned.1.call-done = f32[416,256]{1,0:T(8,128)} async-done(((f32[416,256]{1,0:T(8,128)}), f32[416,256]{1,0:T(8,128)}) %all-reduce.3.cloned.1.call-update) | async-done | bytes 426000 | tf_op jit(solution)/shard_map/psum | solution.py:95
  62.9 2.8 fusion.4
  65.8 0.0 all-reduce.5.cloned.1.call-update
  65.8 0.0 reduce-scatter.2.cloned.1.call-start
  65.8 10.1 %fusion.2 = f32[2048,256]{1,0:T(8,128)} fusion(f32[416,256]{1,0:T(8,128)} %all-reduce.3.cloned.1.call-done, f32[416,2048]{1,0:T(8,128)} %param.4, bf16[416,2048]{1,0:T(8,128)(2,1)S(1)} %copy-done.3), kind=kOutput, calls=%fused_computation.7 | convolution fusion | flops 2618949632 | bytes 7634944 | tf_op jit(solution)/shard_map/dot_general | solution.py:15
  76.0 0.2 all-gather.2.cloned.1.call-start
  76.2 169.2 %all-reduce.5.cloned.1.call-done.gram_ref = f32[256,256]{1,0:T(8,128)} async-done(((f32[256,256]{1,0:T(8,128)}), f32[256,256]{1,0:T(8,128)}) %all-reduce.5.cloned.1.call-update) | async-done | bytes 262160 | tf_op jit(solution)/shard_map/psum | solution.py:96
  245.4 0.9 copy-done.1
  246.4 8.6 %shard_map.58 = f32[256,256]{1,0:T(8,128)S(1)} custom-call(f32[256,256]{1,0:T(8,128)S(1)} %copy-done.1), custom_call_target="tpu_custom_call" | custom-call | tf_op jit(solution)/shard_map/pallas_call | solution.py:82
  254.9 127.9 %reduce-scatter.2.cloned.1.call-done = f32[32,256]{1,0:T(8,128)} async-done(((f32[2048,256]{1,0:T(8,128)}), f32[32,256]{1,0:T(8,128)}) %reduce-scatter.2.cloned.1.call-update) | async-done | bytes 32784 | tf_op jit(solution)/shard_map/reduce_scatter | solution.py:98
  382.8 1.7 convolution_convert_fusion.1
  384.5 0.0 all-gather.2.cloned.1.call-update
  384.6 1.2 convolution_convert_fusion
  385.8 80.8 %all-gather.2.cloned.1.call-done = bf16[2048,256]{1,0:T(8,128)(2,1)} async-done(((bf16[32,256]{1,0:T(8,128)(2,1)}), bf16[2048,256]{1,0:T(8,128)(2,1)}) %all-gather.2.cloned.1.call-update) | async-done | bytes 1048592 | tf_op jit(solution)/shard_map/all_gather | solution.py:102
  466.6 1.5 fusion
  468.2 8.4 %psum.23 = f32[256]{0:T(256)S(1)} all-reduce(f32[256]{0:T(256)S(1)} %fusion), channel_id=1, replica_groups=mesh['fsdp'=64,'tensor'=4] {'tensor'}, use_global_device_ids=true, to_apply=%region_4.0 | all-reduce | flops 256 | bytes 2048 | tf_op jit(solution)/shard_map/psum | solution.py:104
  476.6 1.6 fusion.1
  478.2 3.2 multiply_convert_fusion
  481.4 2.5 multiply_subtract_fusion
  (16 shorter events, 0.1 us)
Async XLA Ops:
  7.2 1.2 copy-start
  7.2 58.7 %copy-start.3 = (bf16[416,2048]{1,0:T(8,128)(2,1)S(1)}, bf16[416,2048]{1,0:T(8,128)(2,1)}, u32[]{:S(2)}) copy-start(bf16[416,2048]{1,0:T(8,128)(2,1)} %param.3) | copy-start | bytes 5111812
  7.2 55.7 %all-reduce.3.cloned.1.call-start = ((), (), s32[]{:S(2)}) async-start(), calls=%async_computation.1 | async-start | bytes 851968 | tf_op jit(solution)/shard_map/psum | solution.py:95
  13.5 232.0 %all-reduce.5.cloned.1.call-start = ((), (), s32[]{:S(2)}) async-start(), calls=%async_computation.2 | async-start | bytes 524288 | tf_op jit(solution)/shard_map/psum | solution.py:96
  65.8 318.8 %copy-start.5 = (f32[416,256]{1,0:T(8,128)S(1)}, f32[416,256]{1,0:T(8,128)}, u32[]{:S(2)}) copy-start(f32[416,256]{1,0:T(8,128)} %all-reduce.3.cloned.1.call-done) | copy-start | bytes 1277956
  65.8 317.0 %reduce-scatter.2.cloned.1.call-start = ((), (), s32[]{:S(2)}) async-start(), calls=%async_computation.3 | async-start | bytes 2129920 | tf_op jit(solution)/shard_map/reduce_scatter | solution.py:98
  76.0 390.6 %all-gather.2.cloned.1.call-start = ((), (), s32[]{:S(2)}) async-start(), calls=%async_computation.4 | async-start | bytes 1064960 | tf_op jit(solution)/shard_map/all_gather | solution.py:102
  245.4 0.9 copy-start.1
  385.8 95.6 %copy-start.7 = (bf16[416,256]{1,0:T(8,128)(2,1)S(1)}, bf16[416,256]{1,0:T(8,128)(2,1)}, u32[]{:S(2)}) copy-start(bf16[416,256]{1,0:T(8,128)(2,1)} %convolution_convert_fusion) | copy-start | bytes 638980
  476.6 4.8 copy-start.2
  476.6 4.8 copy-start.4
  478.2 5.7 %copy-start.6 = (bf16[2048,256]{1,0:T(8,128)(2,1)}, bf16[2048,256]{1,0:T(8,128)(2,1)S(1)}, u32[]{:S(2)}) copy-start(bf16[2048,256]{1,0:T(8,128)(2,1)S(1)} %fusion.1) | copy-start | bytes 3145732
Sparse Core Ops, SparseCore 0:
  13.6 49.2 all-reduce.2
  67.4 178.0 all-reduce.4
  250.0 132.7 reduce-scatter.1
  386.4 80.1 all-gather.1

commit v2 on v1

--- a/solution.py
+++ b/solution.py
@@ -1,3 +1,4 @@
+import functools
 import math
 
 import jax
@@ -7,6 +8,8 @@
 from jax.experimental.pallas import tpu as pltpu
 from jax.sharding import PartitionSpec as P
 
+MESH = pl.DeviceIdType.MESH
+BF16 = jnp.bfloat16
 HIGH = lax.Precision.HIGHEST
 F32 = jnp.float32
 
@@ -78,38 +81,361 @@
     out_ref[half:, half:] = second
 
 
-def factor(gram):
+def fast_dot(a, b, dims):
+    return lax.dot_general(a, b, (dims, ((), ())), preferred_element_type=F32)
+
+
+def two_parts(value):
+    upper = value.astype(BF16)
+    return upper, (value - upper.astype(F32)).astype(BF16)
+
+
+def put(src, dst, send, recv, **where):
+    copy = pltpu.make_async_remote_copy(
+        src_ref=src, dst_ref=dst, send_sem=send, recv_sem=recv, device_id=where, device_id_type=MESH
+    )
+    copy.start()
+    return copy
+
+
+def place():
+    flat = lax.axis_index("fsdp")
+    return flat // 8, flat % 8 // 2, flat % 2, lax.axis_index("tensor")
+
+
+def at(z, x, core):
+    return z * 8 + x * 2 + core
+
+
+def greet(others):
+    barrier = pltpu.get_barrier_semaphore()
+    for where in others:
+        pl.semaphore_signal(barrier, inc=1, device_id=where, device_id_type=MESH)
+    return lambda: pl.semaphore_wait(barrier, len(others))
+
+
+ORDER = (2, 1, 3, 0)
+
+
+def sums_kernel(
+    grad_hbm, momentum_hbm, basis_hbm,
+    panel, gram, shard,
+    grad_in, momentum_in, basis_in, high, low, piece, panel_got,
+    quarter, gram_got, gram_z, cross, cross_got, lane_sent, lane_got, block, block_got,
+    load_sem, ysend, yrecv, gsend, grecv, csend, crecv, xsend, xrecv, zsend, zrecv,
+):
+    z, x, core, y = place()
+    b = x * 2 + core
+    rows = grad_hbm.shape[0]
+    fourth = rows // 4
+    taller = fourth + 8
+    others = [{"tensor": (y + o) % 4} for o in (1, 2, 3)]
+    others += [{"fsdp": z * 8 + (b + o) % 8} for o in range(1, 8)]
+    others += [{"fsdp": (z + o) % 8 * 8 + b} for o in range(1, 8)]
+    greeted = greet(others)
+    basis_load = pltpu.make_async_copy(basis_hbm, basis_in, load_sem.at[8])
+    basis_load.start()
+    loads = []
+    for n, o in enumerate(ORDER):
+        p = (y + o) % 4
+        start = pl.multiple_of(p * fourth - 8 * (p % 2), 16)
+        for which, (src, dst) in enumerate(((grad_hbm, grad_in), (momentum_hbm, momentum_in))):
+            load = pltpu.make_async_copy(src.at[pl.ds(start, taller)], dst.at[n], load_sem.at[2 * n + which])
+            load.start()
+            loads.append(load)
+    basis_load.wait()
+    copies = []
+    for n, o in enumerate(ORDER):
+        p = (y + o) % 4
+        start = pl.multiple_of(p * fourth - 8 * (p % 2), 16)
+        skip = pl.multiple_of(8 * (p % 2), 8)
+        loads[2 * n].wait()
+        loads[2 * n + 1].wait()
+        upper, lower = two_parts(momentum_in[n] + grad_in[n].astype(F32))
+        high[pl.ds(start, taller), :] = upper
+        low[pl.ds(start, taller), :] = lower
+        basis_v = basis_in[...]
+        piece[n] = fast_dot(upper, basis_v, ((1,), (0,))) + fast_dot(lower, basis_v, ((1,), (0,)))
+        if n == 0:
+            greeted()
+        if o:
+            copies.append(put(piece.at[n, pl.ds(skip, fourth)], panel_got.at[o - 1], ysend.at[o - 1], yrecv.at[o - 1], tensor=p))
+    skip = pl.multiple_of(8 * (y % 2), 8)
+    total = piece[3, pl.ds(skip, fourth), :]
+    for copy in copies:
+        copy.wait_recv()
+    for o in (1, 2, 3):
+        total = total + panel_got[o - 1]
+    mine = pl.ds(pl.multiple_of(y * fourth, 8), fourth)
+    panel[mine, :] = total
+    gathers = [
+        put(panel.at[mine], panel.at[mine], ysend.at[2 + o], yrecv.at[2 + o], tensor=(y + o) % 4) for o in (1, 2, 3)
+    ]
+    for copy in gathers:
+        copy.wait_recv()
+    copies += gathers
+
+    whole = panel[...]
+    wide = panel[:, pl.ds(pl.multiple_of(y // 2 * 128, 128), 128)]
+    quarter[...] = dot(wide, whole, ((0,), (0,)))
+    first = y % 2 * 64
+    rounds = []
+    for o in range(1, 8):
+        to = (b + o) % 8
+        rounds.append(
+            put(quarter.at[pl.ds(pl.multiple_of(first + to * 8, 8), 8)], gram_got.at[o - 1],
+                gsend.at[0, o - 1], grecv.at[0, o - 1], fsdp=z * 8 + to)
+        )
+
+    panel_high, panel_low = two_parts(whole)
+
+    def product(start):
+        upper = high[:, pl.ds(pl.multiple_of(start, 256), 256)]
+        lower = low[:, pl.ds(pl.multiple_of(start, 256), 256)]
+        return (
+            fast_dot(upper, panel_high, ((0,), (0,)))
+            + fast_dot(lower, panel_high, ((0,), (0,)))
+            + fast_dot(upper, panel_low, ((0,), (0,)))
+        )
+
+    crossing = []
+    for n, o in enumerate(ORDER):
+        cross[n] = product((1 - core) * 1024 + (x + o) % 4 * 256)
+        crossing.append(put(cross.at[n], cross_got.at[n], csend.at[n], crecv.at[n], fsdp=at(z, x, 1 - core)))
+
+    for copy in rounds:
+        copy.wait_recv()
+    total = quarter[pl.ds(pl.multiple_of(first + b * 8, 8), 8), :]
+    for o in range(1, 8):
+        total = total + gram_got[o - 1]
+    gram_z[z] = total
+    copies += rounds
+    rounds = [
+        put(gram_z.at[z], gram_z.at[z], gsend.at[1, o - 1], grecv.at[1, o - 1], fsdp=(z + o) % 8 * 8 + b)
+        for o in range(1, 8)
+    ]
+
+    passing = []
+    for n, o in enumerate(ORDER):
+        own = product(core * 1024 + (x + o) % 4 * 256)
+        crossing[n].wait_recv()
+        lane_sent[n] = own + cross_got[n]
+        if o:
+            passing.append(
+                put(lane_sent.at[n], lane_got.at[o - 1], xsend.at[o - 1], xrecv.at[o - 1], fsdp=at(z, (x + o) % 4, core))
+            )
+
+    for copy in rounds:
+        copy.wait_recv()
+    total = gram_z[0]
+    for n in range(1, 8):
+        total = total + gram_z[n]
+    here = pl.ds(pl.multiple_of(y * 64 + b * 8, 8), 8)
+    gram[here, :] = total
+    copies += rounds
+    rounds = [
+        put(gram.at[here], gram.at[here], gsend.at[2, o - 1], grecv.at[2, o - 1], fsdp=z * 8 + (b + o) % 8)
+        for o in range(1, 8)
+    ]
+    for copy in rounds:
+        copy.wait_recv()
+    copies += rounds
+    here = pl.ds(pl.multiple_of(y * 64, 64), 64)
+    rounds = [
+        put(gram.at[here], gram.at[here], gsend.at[3, o - 1], grecv.at[3, o - 1], tensor=(y + o) % 4) for o in (1, 2, 3)
+    ]
+
+    for copy in passing:
+        copy.wait_recv()
+    block[...] = lane_sent[3] + lane_got[0] + lane_got[1] + lane_got[2]
+    last = []
+    for o in range(1, 8):
+        to = (z + o) % 8
+        last.append(
+            put(block.at[pl.ds(pl.multiple_of(to * 32, 32), 32)], block_got.at[o - 1], zsend.at[o - 1], zrecv.at[o - 1],
+                fsdp=at(to, x, core))
+        )
+    for copy in rounds:
+        copy.wait_recv()
+    copies += rounds
+    for copy in last:
+        copy.wait_recv()
+    total = block[pl.ds(pl.multiple_of(z * 32, 32), 32), :]
+    for n in range(7):
+        total = total + block_got[n]
+    shard[...] = total
+    for copy in copies + crossing + passing + last:
+        copy.wait_send()
+
+
+def sums(grad, momentum, basis):
+    rows, cols = grad.shape
+    rank = basis.shape[1]
+    fourth = rows // 4
+    dma = pltpu.SemaphoreType.DMA
     return pl.pallas_call(
-        factor_kernel,
-        out_shape=jax.ShapeDtypeStruct(gram.shape, F32),
+        sums_kernel,
+        out_shape=(
+            jax.ShapeDtypeStruct((rows, rank), F32),
+            jax.ShapeDtypeStruct((rank, rank), F32),
+            jax.ShapeDtypeStruct((cols // 64, rank), F32),
+        ),
+        in_specs=[pl.BlockSpec(memory_space=pl.ANY)] * 3,
+        out_specs=(pl.BlockSpec(memory_space=pltpu.VMEM),) * 3,
+        scratch_shapes=[
+            pltpu.VMEM((4, fourth + 8, cols), BF16),
+            pltpu.VMEM((4, fourth + 8, cols), F32),
+            pltpu.VMEM((cols, rank), BF16),
+            pltpu.VMEM((rows, cols), BF16),
+            pltpu.VMEM((rows, cols), BF16),
+            pltpu.VMEM((4, fourth + 8, rank), F32),
+            pltpu.VMEM((3, fourth, rank), F32),
+            pltpu.VMEM((128, rank), F32),
+            pltpu.VMEM((7, 8, rank), F32),
+            pltpu.VMEM((8, 8, rank), F32),
+            pltpu.VMEM((4, 256, rank), F32),
+            pltpu.VMEM((4, 256, rank), F32),
+            pltpu.VMEM((4, 256, rank), F32),
+            pltpu.VMEM((3, 256, rank), F32),
+            pltpu.VMEM((256, rank), F32),
+            pltpu.VMEM((7, 32, rank), F32),
+            dma((9,)), dma((6,)), dma((6,)), dma((4, 7)), dma((4, 7)), dma((4,)), dma((4,)),
+            dma((3,)), dma((3,)), dma((7,)), dma((7,)),
+        ],
+        compiler_params=pltpu.CompilerParams(collective_id=0, has_side_effects=True, vmem_limit_bytes=48 << 20),
+    )(grad, momentum, basis)
+
+
+def solve_kernel(gram_ref, panel_ref, shard_ref, ortho_ref, out_ref, inverse):
+    factor_kernel(gram_ref, inverse)
+    out_ref[...] = dot(shard_ref[...], inverse[...], ((1,), (1,))).astype(BF16)
+    ortho_ref[...] = dot(panel_ref[...], inverse[...], ((1,), (1,))).astype(BF16)
+
+
+def solve(gram, panel, shard):
+    return pl.pallas_call(
+        solve_kernel,
+        out_shape=(jax.ShapeDtypeStruct(panel.shape, BF16), jax.ShapeDtypeStruct(shard.shape, BF16)),
+        in_specs=[pl.BlockSpec(memory_space=pltpu.VMEM)] * 3,
+        out_specs=(pl.BlockSpec(memory_space=pltpu.VMEM),) * 2,
+        scratch_shapes=[pltpu.VMEM(gram.shape, F32)],
+        compiler_params=pltpu.CompilerParams(vmem_limit_bytes=32 << 20),
+    )(gram, panel, shard)
+
+
+def gather_kernel(shard, rounded, scales, squares, zsend, zrecv, xsend, xrecv, csend, crecv, ysend, yrecv):
+    z, x, core, y = place()
+    others = [{"fsdp": at((z + o) % 8, x, core)} for o in range(1, 8)]
+    others += [{"fsdp": at(z, (x + o) % 4, core)} for o in (1, 2, 3)]
+    others += [{"fsdp": at(z, x, 1 - core)}]
+    others += [{"tensor": (y + o) % 4} for o in (1, 2, 3)]
+    greeted = greet(others)
+
+    def rows_of(z_of):
+        return pl.ds(pl.multiple_of(core * 1024 + x * 256 + z_of * 32, 32), 32)
+
+    rounded[rows_of(z), :] = shard[...]
+    greeted()
+    here = rows_of(z)
+    along_z = [
+        put(rounded.at[here], rounded.at[here], zsend.at[o - 1], zrecv.at[o - 1], fsdp=at((z + o) % 8, x, core))
+        for o in range(1, 8)
+    ]
+    along_x = []
+    for zo in range(8):
+        here = rows_of((z + 8 - zo) % 8)
+        if zo:
+            along_z[zo - 1].wait_recv()
+        for o in (2, 1, 3):
+            along_x.append(
+                put(rounded.at[here], rounded.at[here], xsend.at[o - 1, zo], xrecv.at[o - 1, zo],
+                    fsdp=at(z, (x + o) % 4, core))
+            )
+    across = []
+    for o in (0, 1, 3, 2):
+        if o:
+            for zo in range(8):
+                along_x[3 * zo + (2, 1, 3).index(o)].wait_recv()
+        here = pl.ds(pl.multiple_of(core * 1024 + (x + 4 - o) % 4 * 256, 256), 256)
+        across.append(put(rounded.at[here], rounded.at[here], csend.at[o], crecv.at[o], fsdp=at(z, x, 1 - core)))
+    for copy in across:
+        copy.wait_recv()
+    total = jnp.zeros((8, rounded.shape[1]), F32)
+    for n in range(8):
+        part = rounded[256 * n : 256 * n + 256, :].astype(F32)
+        part = part * part
+        for i in range(32):
+            total = total + part[8 * i : 8 * i + 8, :]
+    squares[y] = total
+    along_y = [
+        put(squares.at[y], squares.at[y], ysend.at[o - 1], yrecv.at[o - 1], tensor=(y + o) % 4) for o in (1, 2, 3)
+    ]
+    for copy in along_y:
+        copy.wait_recv()
+    total = squares[0] + squares[1] + squares[2] + squares[3]
+    total = jnp.sum(total, axis=0, keepdims=True)
+    scales[...] = jnp.broadcast_to(lax.rsqrt(total + 1e-06), scales.shape)
+    for copy in along_z + along_x + across + along_y:
+        copy.wait_send()
+
+
+def gather(shard):
+    rank = shard.shape[1]
+    dma = pltpu.SemaphoreType.DMA
+    return pl.pallas_call(
+        gather_kernel,
+        out_shape=(
+            jax.ShapeDtypeStruct((64 * shard.shape[0], rank), BF16),
+            jax.ShapeDtypeStruct((8, rank), F32),
+        ),
         in_specs=[pl.BlockSpec(memory_space=pltpu.VMEM)],
-        out_specs=pl.BlockSpec(memory_space=pltpu.VMEM),
+        out_specs=(pl.BlockSpec(memory_space=pltpu.VMEM),) * 2,
+        scratch_shapes=[
+            pltpu.VMEM((4, 8, rank), F32),
+            dma((7,)), dma((7,)), dma((3, 8)), dma((3, 8)), dma((4,)), dma((4,)), dma((3,)), dma((3,)),
+        ],
+        compiler_params=pltpu.CompilerParams(collective_id=1, has_side_effects=True, vmem_limit_bytes=32 << 20),
+    )(shard)
+
+
+def finish_kernel(scale, grad, momentum, ortho, rounded, scales, new_momentum, update, basis_next):
+    columns = rounded[...]
+    following = (columns.astype(F32) * scales[:1, :]).astype(BF16)
+    basis_next[...] = following
+    blended = momentum[...] + grad[...].astype(F32)
+    new_momentum[...] = blended - 0.05 * fast_dot(ortho[...], columns, ((1,), (1,)))
+    update[...] = (scale * fast_dot(ortho[...], following, ((1,), (1,)))).astype(BF16)
+
+
+def finish(scale, grad, momentum, ortho, rounded, scales):
+    rows, cols = grad.shape
+    rank = ortho.shape[1]
+    wide = 256
+    part = pl.BlockSpec((rows, wide), lambda i: (0, i))
+    tall = pl.BlockSpec((wide, rank), lambda i: (i, 0))
+    return pl.pallas_call(
+        functools.partial(finish_kernel, scale),
+        grid=(cols // wide,),
+        out_shape=(
+            jax.ShapeDtypeStruct((rows, cols), F32),
+            jax.ShapeDtypeStruct((rows, cols), BF16),
+            jax.ShapeDtypeStruct((cols, rank), BF16),
+        ),
+        in_specs=[
+            part, part, pl.BlockSpec((rows, rank), lambda i: (0, 0)), tall, pl.BlockSpec((8, rank), lambda i: (0, 0)),
+        ],
+        out_specs=(part, part, tall),
         compiler_params=pltpu.CompilerParams(vmem_limit_bytes=32 << 20),
-    )(gram)
+    )(grad, momentum, ortho, rounded, scales)
 
 
 def on_device(grad, momentum, basis):
     rows_here, cols_here = grad.shape
-    rank = basis.shape[1]
-    blended = momentum + grad.astype(F32)
-    panel = lax.psum(dot(blended, basis.astype(F32), ((1,), (0,))), "tensor")
-    gram = lax.psum(dot(panel, panel, ((0,), (0,))), "fsdp")
-    partial = dot(blended, panel, ((0,), (0,)))
-    mine = lax.psum_scatter(partial, "fsdp", scatter_dimension=0, tiled=True)
-    inverse = factor(gram)
-    ortho = dot(panel, inverse, ((1,), (1,)))
-    shard = dot(mine, inverse, ((1,), (1,))).astype(jnp.bfloat16)
-    rounded = lax.all_gather(shard, "fsdp", axis=0, tiled=True)
-    rounded_f = rounded.astype(F32)
-    column_sq = lax.psum(jnp.sum(rounded_f * rounded_f, axis=0), "tensor")
-    basis_next = (rounded_f * lax.rsqrt(column_sq + 1e-06)[None, :]).astype(jnp.bfloat16)
-    ortho_b = ortho.astype(jnp.bfloat16)
-    back = lax.dot_general(ortho_b, rounded, (((1,), (1,)), ((), ())), preferred_element_type=F32)
-    new_momentum = blended - 0.05 * back
-    scale = math.sqrt(rows_here * lax.axis_size("fsdp") * cols_here * lax.axis_size("tensor") / rank)
-    step = lax.dot_general(ortho_b, basis_next, (((1,), (1,)), ((), ())), preferred_element_type=F32)
-    update = (scale * step).astype(jnp.bfloat16)
-    return (new_momentum, update, basis_next)
+    scale = math.sqrt(rows_here * lax.axis_size("fsdp") * cols_here * lax.axis_size("tensor") / basis.shape[1])
+    panel, gram, shard = sums(grad, momentum, basis)
+    ortho, shard = solve(gram, panel, shard)
+    rounded, scales = gather(shard)
+    return finish(scale, grad, momentum, ortho, rounded, scales)
 
 
 def solution(mesh):

time: 491 us -> 91.1 us (0.19)
  waiting for transfers between devices: 427 us -> 0 us
  Pallas kernels: 8.56 us -> 87.4 us
  matrix products: 26.6 us -> 0 us
  between operations: 13.8 us -> 0.68 us
  blocking collectives: 8.45 us -> 0 us
    psum x2 -> x0, waiting for transfers between devices: 219 us -> none  [the longest x1 169 us: on_device(): gram = lax.psum(dot(panel, panel, ((0,), (0,))), 'fsdp')]
    reduce_scatter x1 -> x0, waiting for transfers between devices: 128 us -> none  [on_device(): mine = lax.psum_scatter(partial, 'fsdp', scatter_dimension=0, tiled=True)]
    all_gather x1 -> x0, waiting for transfers between devices: 80.8 us -> none  [on_device(): rounded = lax.all_gather(shard, 'fsdp', axis=0, tiled=True)]
    pallas_call x1 -> x4, Pallas kernels: 8.56 us -> 87.4 us  [the longest x1 51.2 us: sums(): pl.pallas_call(sums_kernel, out_shape=(jax.ShapeDtypeStruct((rows, rank),...]
    dot_general x7 -> x0, matrix products: 26.6 us -> none  [the longest x5 20.9 us: dot(): lax.dot_general(a, b, (dims, ((), ())), precision=HIGH, preferred_element...]
    psum x1 -> x0, blocking collectives: 8.45 us -> none  [on_device(): column_sq = lax.psum(jnp.sum(rounded_f * rounded_f, axis=0), 'tensor')]
  transfers between devices with their start and end apart: 4 -> 0, of which waited for: 4 -> 0; matrix products, arithmetic and copies ran while one was open for 2% -> 0% of each run, Pallas kernels for 2% -> 0%
where the time goes in v2:
time: 91.1 us; the launch traced here: 90.9 us
  Pallas kernels  87.4 us (96%)
  local copies, waits for them, and re-layouts  2.83 us (3%)
    pallas_call x1, Pallas kernels, sums(): pl.pallas_call(sums_kernel, out_shape=(jax.ShapeDtypeStruct((rows, rank),...  51.2 us
    pallas_call x1, Pallas kernels, gather(): pl.pallas_call(gather_kernel, out_shape=(jax.ShapeDtypeStruct((64 * shard...  21.3 us
    pallas_call x1, Pallas kernels, solve(): pl.pallas_call(solve_kernel, out_shape=(jax.ShapeDtypeStruct(panel.shape,...  9.63 us
    pallas_call x1, Pallas kernels, finish(): pl.pallas_call(functools.partial(finish_kernel, scale), grid=(cols // wid...  5.37 us
    unnamed x6, local copies, waits for them, and re-layouts  2.83 us

profile of v2, /device:TPU:1, one launch (start us, length us, event | category | flops | bytes accessed | tf_op | source)
XLA Modules:
  0.0 90.9 jit_solution(9761832189758449494)
XLA Ops:
  0.6 0.0 copy-start
  0.6 0.0 copy-start.1
  0.7 1.6 %copy-done.1 = bf16[416,2048]{1,0:T(8,128)(2,1)S(1)} copy-done((bf16[416,2048]{1,0:T(8,128)(2,1)S(1)}, bf16[416,2048]{1,0:T(8,128)(2,1)}, u32[]{:S(2)}) %copy-start.1) | copy-done | bytes 1703960
  2.2 0.0 copy-start.2
  2.2 1.2 %copy-done.2 = bf16[2048,256]{1,0:T(8,128)(2,1)S(1)} copy-done((bf16[2048,256]{1,0:T(8,128)(2,1)S(1)}, bf16[2048,256]{1,0:T(8,128)(2,1)}, u32[]{:S(2)}) %copy-start.2) | copy-done | bytes 1048600
  3.5 51.2 %shard_map.58 = (f32[416,256]{1,0:T(8,128)S(1)}, f32[256,256]{1,0:T(8,128)S(1)}, f32[32,256]{1,0:T(8,128)S(1)}) custom-call(bf16[416,2048]{1,0:T(8,128)(2,1)S(1)} %copy-done.1, f32[416,2048]{1,0:T(8,128)} %momentum.1, bf16[2048,256]{1,0:T(8,128)(2,1)S(1)} %copy-done.2), custom_call_target="tpu_custom_call" | custom-call | tf_op jit(solution)/shard_map/pallas_call | solution.py:276
  54.7 9.6 %shard_map.59 = (bf16[416,256]{1,0:T(8,128)(2,1)S(1)}, bf16[32,256]{1,0:T(8,128)(2,1)S(1)}) custom-call(f32[256,256]{1,0:T(8,128)S(1)} %get-tuple-element.10.gram_ref, f32[416,256]{1,0:T(8,128)S(1)} %get-tuple-element.11.panel_ref, f32[32,256]{1,0:T(8,128)S(1)} %get-tuple-element.12.shard_ref), custom_call_target="tpu_custom_call" | custom-call | tf_op jit(solution)/shard_map/pallas_call | solution.py:316
  64.3 21.3 %shard_map.60 = (bf16[2048,256]{1,0:T(8,128)(2,1)S(1)}, f32[8,256]{1,0:T(8,128)S(1)}) custom-call(bf16[32,256]{1,0:T(8,128)(2,1)S(1)} %get-tuple-element.14.shard), custom_call_target="tpu_custom_call" | custom-call | tf_op jit(solution)/shard_map/pallas_call | solution.py:385
  85.6 0.0 copy-done
  85.6 5.4 %shard_map.61 = (f32[416,2048]{1,0:T(8,128)}, bf16[416,2048]{1,0:T(8,128)(2,1)}, bf16[2048,256]{1,0:T(8,128)(2,1)}) custom-call(bf16[416,2048]{1,0:T(8,128)(2,1)S(1)} %copy-done.1, f32[416,2048]{1,0:T(8,128)S(1)} %copy-done, bf16[416,256]{1,0:T(8,128)(2,1)S(1)} %get-tuple-element.13.ortho, bf16[2048,256]{1,0:T(8,128)(2,1)S(1)} %get-tuple-element.15.rounded, ...), custom_call_target="tpu_custom_call" | custom-call | tf_op jit(solution)/shard_map/pallas_call | solution.py:416
Async XLA Ops:
  0.6 84.9 %copy-start = (f32[416,2048]{1,0:T(8,128)S(1)}, f32[416,2048]{1,0:T(8,128)}, u32[]{:S(2)}) copy-start(f32[416,2048]{1,0:T(8,128)} %momentum.1) | copy-start | bytes 10223620
  0.6 1.6 %copy-start.1 = (bf16[416,2048]{1,0:T(8,128)(2,1)S(1)}, bf16[416,2048]{1,0:T(8,128)(2,1)}, u32[]{:S(2)}) copy-start(bf16[416,2048]{1,0:T(8,128)(2,1)} %grad.1) | copy-start | bytes 5111812
  2.2 1.2 %copy-start.2 = (bf16[2048,256]{1,0:T(8,128)(2,1)S(1)}, bf16[2048,256]{1,0:T(8,128)(2,1)}, u32[]{:S(2)}) copy-start(bf16[2048,256]{1,0:T(8,128)(2,1)} %basis_hbm.1) | copy-start | bytes 3145732

commit v3 on v2

v3 whole, which is shorter than its diff:
```python
import functools
import math

import jax
import jax.numpy as jnp
from jax import lax
from jax.experimental import pallas as pl
from jax.experimental.pallas import tpu as pltpu
from jax.sharding import PartitionSpec as P

MESH = pl.DeviceIdType.MESH
BF16 = jnp.bfloat16
HIGH = lax.Precision.HIGHEST
F32 = jnp.float32


def dot(a, b, dims):
    return lax.dot_general(a, b, (dims, ((), ())), precision=HIGH, preferred_element_type=F32)


def inverse_factor(square):
    size = square.shape[0]
    tall = size // 8
    tiles = [square[8 * i : 8 * i + 8, :] for i in range(tall)]
    lane = lax.broadcasted_iota(jnp.int32, (8, size), 1)
    sub = lax.broadcasted_iota(jnp.int32, (8, size), 0)
    pivots = []
    for t in range(tall):
        start = 8 * t
        left = tall - t
        cols = [
            [jnp.broadcast_to(tiles[i][:, start + l : start + l + 1], (8, size)) for i in range(t, tall)]
            for l in range(8)
        ]
        mult = [[None] * left for _ in range(8)]
        group = tiles[t]
        rows = []
        pivot = jnp.zeros((8, size), F32)
        for l in range(8):
            here = cols[l][0][l : l + 1, :]
            recip = jnp.broadcast_to(1.0 / here, (8, size))
            pivot = jnp.where(sub == l, here, pivot)
            mult[l][0] = jnp.where(sub > l, cols[l][0] * recip, 0.0)
            for i in range(1, left):
                mult[l][i] = cols[l][i] * recip
            for later in range(l + 1, 8):
                across = jnp.broadcast_to(cols[later][0][l : l + 1, :], (8, size))
                for i in range(left):
                    cols[later][i] = cols[later][i] - mult[l][i] * across
            at = start + l
            row = jnp.where(lane[:1] == at, 1.0, group[l : l + 1, :])
            group = jnp.where((lane == at) & (sub > l), 0.0, group)
            group = group - mult[l][0] * jnp.broadcast_to(row, (8, size))
            row = jnp.where((lane[:1] > at) & (lane[:1] < start + 8), 0.0, row)
            rows.append(jnp.broadcast_to(row, (8, size)))
        tiles[t] = group
        pivots.append(pivot)
        for i in range(1, left):
            total = mult[0][i] * rows[0]
            for l in range(1, 8):
                total = total + mult[l][i] * rows[l]
            kept = jnp.where((lane >= start) & (lane < start + 8), 0.0, tiles[t + i])
            tiles[t + i] = kept - total
    out = []
    for i in range(tall):
        at = sub + 8 * i
        unit = jnp.where(lane == at, 1.0, jnp.where(lane < at, tiles[i], 0.0))
        out.append(unit * lax.rsqrt(pivots[i]))
    return jnp.concatenate(out, 0)


def factor_kernel(gram_ref, out_ref):
    half = gram_ref.shape[0] // 2
    first = inverse_factor(gram_ref[:half, :half])
    across = dot(first, gram_ref[:half, half:], ((1,), (0,)))
    second = inverse_factor(gram_ref[half:, half:] - dot(across, across, ((0,), (0,))))
    below = -dot(across, first, ((0,), (0,)))
    out_ref[:half, :half] = first
    out_ref[:half, half:] = jnp.zeros((half, half), F32)
    out_ref[half:, :half] = dot(second, below, ((1,), (0,)))
    out_ref[half:, half:] = second


def fast_dot(a, b, dims):
    return lax.dot_general(a, b, (dims, ((), ())), preferred_element_type=F32)


def two_parts(value):
    upper = value.astype(BF16)
    return upper, (value - upper.astype(F32)).astype(BF16)


def put(src, dst, send, recv, **where):
    copy = pltpu.make_async_remote_copy(
        src_ref=src, dst_ref=dst, send_sem=send, recv_sem=recv, device_id=where, device_id_type=MESH
    )
    copy.start()
    return copy


def place():
    flat = lax.axis_index("fsdp")
    return flat // 8, flat % 8 // 2, flat % 2, lax.axis_index("tensor")


def at(z, x, core):
    return z * 8 + x * 2 + core


def greet(others):
    barrier = pltpu.get_barrier_semaphore()
    for where in others:
        pl.semaphore_signal(barrier, inc=1, device_id=where, device_id_type=MESH)
    return lambda: pl.semaphore_wait(barrier, len(others))


ORDER = (2, 1, 3, 0)
ALONG_YX = tuple((oy, ox) for oy in range(4) for ox in range(4) if oy or ox)


def main_kernel(
    grad_hbm, momentum_hbm, basis_hbm,
    rounded, ortho, scales,
    grad_in, momentum_in, basis_in, high, low, piece, panel_got, panel,
    gram_own, gram_half, gram_got, gram_z, gram, inverse,
    cross, cross_got, lane_sent, lane_got, block, block_got, squares, halves,
    load_sem, ysend, yrecv, gsend, grecv, zgsend, zgrecv, g2send, g2recv, g3send, g3recv,
    csend, crecv, xsend, xrecv, zsend, zrecv, azsend, azrecv, axsend, axrecv, acsend, acrecv, sqsend, sqrecv,
):
    z, x, core, y = place()
    rows = grad_hbm.shape[0]
    fourth = rows // 4
    taller = fourth + 8
    sibling = at(z, x, 1 - core)
    others = [{"fsdp": at((z + o) % 8, x, core)} for o in range(1, 8)]
    others += [{"fsdp": at(z, (x + ox) % 4, core), "tensor": (y + oy) % 4} for oy, ox in ALONG_YX]
    others += [{"fsdp": sibling}]
    greeted = greet(others)
    basis_load = pltpu.make_async_copy(basis_hbm, basis_in, load_sem.at[8])
    basis_load.start()
    loads = []
    for n, o in enumerate(ORDER):
        p = (y + o) % 4
        start = pl.multiple_of(p * fourth - 8 * (p % 2), 16)
        for which, (src, dst) in enumerate(((grad_hbm, grad_in), (momentum_hbm, momentum_in))):
            load = pltpu.make_async_copy(src.at[pl.ds(start, taller)], dst.at[n], load_sem.at[2 * n + which])
            load.start()
            loads.append(load)
    basis_load.wait()
    sent = []

    def send(src, dst, send_sem, recv_sem, **where):
        copy = put(src, dst, send_sem, recv_sem, **where)
        sent.append(copy)
        return copy

    copies = []
    for n, o in enumerate(ORDER):
        p = (y + o) % 4
        start = pl.multiple_of(p * fourth - 8 * (p % 2), 16)
        skip = pl.multiple_of(8 * (p % 2), 8)
        loads[2 * n].wait()
        loads[2 * n + 1].wait()
        upper, lower = two_parts(momentum_in[n] + grad_in[n].astype(F32))
        high[pl.ds(start, taller), :] = upper
        low[pl.ds(start, taller), :] = lower
        basis_v = basis_in[...]
        piece[n] = fast_dot(upper, basis_v, ((1,), (0,))) + fast_dot(lower, basis_v, ((1,), (0,)))
        if n == 0:
            greeted()
        if o:
            copies.append(send(piece.at[n, pl.ds(skip, fourth)], panel_got.at[o - 1], ysend.at[o - 1], yrecv.at[o - 1], tensor=p))
    skip = pl.multiple_of(8 * (y % 2), 8)
    total = piece[3, pl.ds(skip, fourth), :]
    for copy in copies:
        copy.wait_recv()
    for o in (1, 2, 3):
        total = total + panel_got[o - 1]
    mine = pl.ds(pl.multiple_of(y * fourth, 8), fourth)
    panel[mine, :] = total
    gathers = [
        send(panel.at[mine], panel.at[mine], ysend.at[2 + o], yrecv.at[2 + o], tensor=(y + o) % 4) for o in (1, 2, 3)
    ]

    half = 128
    gram_own[...] = dot(total, total, ((0,), (0,)))
    away = send(gram_own.at[pl.ds(pl.multiple_of((1 - core) * half, half), half)], gram_half, g3send.at[0], g3recv.at[0], fsdp=sibling)
    away.wait_recv()
    kept = pl.ds(pl.multiple_of(core * half, half), half)
    gram_half[...] = gram_half[...] + gram_own[kept, :]
    spread = []
    for n, (oy, ox) in enumerate(ALONG_YX):
        ty, tx = (y + oy) % 4, (x + ox) % 4
        src = gram_half.at[pl.ds(pl.multiple_of((ty * 4 + tx) * 8, 8), 8)]
        spread.append(send(src, gram_got.at[n], gsend.at[n], grecv.at[n], fsdp=at(z, tx, core), tensor=ty))
    for copy in spread:
        copy.wait_recv()
    eight = (y * 4 + x) * 8
    total = gram_half[pl.ds(pl.multiple_of(eight, 8), 8), :]
    for n in range(15):
        total = total + gram_got[n]
    gram_z[z] = total
    around = [
        send(gram_z.at[z], gram_z.at[z], zgsend.at[o - 1], zgrecv.at[o - 1], fsdp=at((z + o) % 8, x, core))
        for o in range(1, 8)
    ]

    for copy in gathers:
        copy.wait_recv()
    panel_high, panel_low = two_parts(panel[...])

    def product(start):
        upper = high[:, pl.ds(pl.multiple_of(start, 256), 256)]
        lower = low[:, pl.ds(pl.multiple_of(start, 256), 256)]
        return (
            fast_dot(upper, panel_high, ((0,), (0,)))
            + fast_dot(lower, panel_high, ((0,), (0,)))
            + fast_dot(upper, panel_low, ((0,), (0,)))
        )

    crossing = []
    for n, o in enumerate(ORDER):
        cross[n] = product((1 - core) * 1024 + (x + o) % 4 * 256)
        crossing.append(send(cross.at[n], cross_got.at[n], csend.at[n], crecv.at[n], fsdp=sibling))
    passing = []
    for n, o in enumerate(ORDER):
        own = product(core * 1024 + (x + o) % 4 * 256)
        crossing[n].wait_recv()
        own = own + cross_got[n]
        if o:
            lane_sent[n] = own.astype(BF16)
            passing.append(
                send(lane_sent.at[n], lane_got.at[o - 1], xsend.at[o - 1], xrecv.at[o - 1], fsdp=at(z, (x + o) % 4, core))
            )
        else:
            block[...] = own

    for copy in around:
        copy.wait_recv()
    total = gram_z[0]
    for n in range(1, 8):
        total = total + gram_z[n]
    here = pl.ds(pl.multiple_of(core * half + eight, 8), 8)
    gram[here, :] = total
    spread = [
        send(gram.at[here], gram.at[here], g2send.at[n], g2recv.at[n], fsdp=at(z, (x + ox) % 4, core), tensor=(y + oy) % 4)
        for n, (oy, ox) in enumerate(ALONG_YX)
    ]
    for copy in spread:
        copy.wait_recv()
    away = send(gram.at[kept], gram.at[kept], g3send.at[1], g3recv.at[1], fsdp=sibling)

    for copy in passing:
        copy.wait_recv()
    block[...] = block[...] + lane_got[0].astype(F32) + lane_got[1].astype(F32) + lane_got[2].astype(F32)
    last = []
    for o in range(1, 8):
        to = (z + o) % 8
        last.append(
            send(block.at[pl.ds(pl.multiple_of(to * 32, 32), 32)], block_got.at[o - 1], zsend.at[o - 1], zrecv.at[o - 1],
                 fsdp=at(to, x, core))
        )
    away.wait_recv()
    factor_kernel(gram, inverse)
    for copy in last:
        copy.wait_recv()
    total = block[pl.ds(pl.multiple_of(z * 32, 32), 32), :]
    for n in range(7):
        total = total + block_got[n]

    def rows_of(z_of):
        return pl.ds(pl.multiple_of(core * 1024 + x * 256 + z_of * 32, 32), 32)

    here = rows_of(z)
    rounded[here, :] = dot(total, inverse[...], ((1,), (1,))).astype(BF16)
    along_z = [
        send(rounded.at[here], rounded.at[here], azsend.at[o - 1], azrecv.at[o - 1], fsdp=at((z + o) % 8, x, core))
        for o in range(1, 8)
    ]
    along_x = [[None] * 8 for _ in range(4)]

    def pass_on(zo):
        here = rows_of((z + 8 - zo) % 8)
        for o in (2, 1, 3):
            along_x[o][zo] = send(
                rounded.at[here], rounded.at[here], axsend.at[o - 1, zo], axrecv.at[o - 1, zo], fsdp=at(z, (x + o) % 4, core)
            )

    pass_on(0)
    ortho[...] = dot(panel[...], inverse[...], ((1,), (1,))).astype(BF16)
    for zo in (1, 7, 2, 6, 3, 5, 4):
        along_z[zo - 1].wait_recv()
        pass_on(zo)

    def block_of(o):
        return pl.ds(pl.multiple_of(core * 1024 + (x + 4 - o) % 4 * 256, 256), 256)

    across = [send(rounded.at[block_of(0)], rounded.at[block_of(0)], acsend.at[0], acrecv.at[0], fsdp=sibling)]
    total = jnp.zeros((8, rounded.shape[1]), F32)
    part = rounded[block_of(0), :].astype(F32)
    part = part * part
    for i in range(32):
        total = total + part[8 * i : 8 * i + 8, :]
    slot = y * 4 + x
    squares[slot] = total
    spread = [
        send(squares.at[slot], squares.at[slot], sqsend.at[n], sqrecv.at[n], fsdp=at(z, (x + ox) % 4, core), tensor=(y + oy) % 4)
        for n, (oy, ox) in enumerate(ALONG_YX)
    ]
    for copy in spread:
        copy.wait_recv()
    total = squares[0]
    for n in range(1, 16):
        total = total + squares[n]
    halves[core] = total
    away = send(halves.at[core], halves.at[core], g3send.at[2], g3recv.at[2], fsdp=sibling)
    for o in (1, 3, 2):
        for copy in along_x[o]:
            copy.wait_recv()
        across.append(send(rounded.at[block_of(o)], rounded.at[block_of(o)], acsend.at[o], acrecv.at[o], fsdp=sibling))
    away.wait_recv()
    total = jnp.sum(halves[0] + halves[1], axis=0, keepdims=True)
    scales[...] = jnp.broadcast_to(lax.rsqrt(total + 1e-06), scales.shape)
    for copy in across:
        copy.wait_recv()
    for copy in sent:
        copy.wait_send()


def main(grad, momentum, basis):
    rows, cols = grad.shape
    rank = basis.shape[1]
    fourth = rows // 4
    dma = pltpu.SemaphoreType.DMA
    vmem = pltpu.VMEM
    pairs = ((6,), (15,), (7,), (15,), (3,), (4,), (3,), (7,), (7,), (3, 8), (4,), (15,))
    return pl.pallas_call(
        main_kernel,
        out_shape=(
            jax.ShapeDtypeStruct((cols, rank), BF16),
            jax.ShapeDtypeStruct((rows, rank), BF16),
            jax.ShapeDtypeStruct((8, rank), F32),
        ),
        in_specs=[pl.BlockSpec(memory_space=pltpu.HBM)] * 3,
        out_specs=(pl.BlockSpec(memory_space=pltpu.VMEM),) * 3,
        scratch_shapes=[
            vmem((4, fourth + 8, cols), BF16),
            vmem((4, fourth + 8, cols), F32),
            vmem((cols, rank), BF16),
            vmem((rows, cols), BF16),
            vmem((rows, cols), BF16),
            vmem((4, fourth + 8, rank), F32),
            vmem((3, fourth, rank), F32),
            vmem((rows, rank), F32),
            vmem((rank, rank), F32),
            vmem((rank // 2, rank), F32),
            vmem((15, 8, rank), F32),
            vmem((8, 8, rank), F32),
            vmem((rank, rank), F32),
            vmem((rank, rank), F32),
            vmem((4, 256, rank), F32),
            vmem((4, 256, rank), F32),
            vmem((3, 256, rank), BF16),
            vmem((3, 256, rank), BF16),
            vmem((256, rank), F32),
            vmem((7, 32, rank), F32),
            vmem((16, 8, rank), F32),
            vmem((2, 8, rank), F32),
            dma((9,)),
            *[dma(shape) for shape in pairs for _ in range(2)],
        ],
        compiler_params=pltpu.CompilerParams(collective_id=0, has_side_effects=True, vmem_limit_bytes=60 << 20),
    )(grad, momentum, basis)


def finish_kernel(scale, grad, momentum, ortho, rounded, scales, new_momentum, update, basis_next):
    columns = rounded[...]
    following = (columns.astype(F32) * scales[:1, :]).astype(BF16)
    basis_next[...] = following
    blended = momentum[...] + grad[...].astype(F32)
    new_momentum[...] = blended - 0.05 * fast_dot(ortho[...], columns, ((1,), (1,)))
    update[...] = (scale * fast_dot(ortho[...], following, ((1,), (1,)))).astype(BF16)


def finish(scale, grad, momentum, ortho, rounded, scales):
    rows, cols = grad.shape
    rank = ortho.shape[1]
    wide = 256
    part = pl.BlockSpec((rows, wide), lambda i: (0, i))
    tall = pl.BlockSpec((wide, rank), lambda i: (i, 0))
    return pl.pallas_call(
        functools.partial(finish_kernel, scale),
        grid=(cols // wide,),
        out_shape=(
            jax.ShapeDtypeStruct((rows, cols), F32),
            jax.ShapeDtypeStruct((rows, cols), BF16),
            jax.ShapeDtypeStruct((cols, rank), BF16),
        ),
        in_specs=[
            part, part, pl.BlockSpec((rows, rank), lambda i: (0, 0)), tall, pl.BlockSpec((8, rank), lambda i: (0, 0)),
        ],
        out_specs=(part, part, tall),
        compiler_params=pltpu.CompilerParams(vmem_limit_bytes=32 << 20),
    )(grad, momentum, ortho, rounded, scales)


def on_device(grad, momentum, basis):
    rows_here, cols_here = grad.shape
    scale = math.sqrt(rows_here * lax.axis_size("fsdp") * cols_here * lax.axis_size("tensor") / basis.shape[1])
    rounded, ortho, scales = main(grad, momentum, basis)
    return finish(scale, grad, momentum, ortho, rounded, scales)


def solution(mesh):
    return jax.shard_map(
        on_device,
        mesh=mesh,
        in_specs=(P("fsdp", "tensor"), P("fsdp", "tensor"), P("tensor", None)),
        out_specs=(P("fsdp", "tensor"), P("fsdp", "tensor"), P("tensor", None)),
        check_vma=False,
    )
```

time: 91.1 us -> 78.8 us (0.86)
  Pallas kernels: 87.4 us -> 73.6 us
  local copies, waits for them, and re-layouts: 2.83 us -> 4.31 us
    pallas_call x3 -> x1, Pallas kernels: 82.1 us -> 68.3 us  [main(): pl.pallas_call(main_kernel, out_shape=(jax.ShapeDtypeStruct((cols, rank),...]
    unnamed x6 -> x10, local copies, waits for them, and re-layouts: 2.83 us -> 4.31 us
where the time goes in v3:
time: 78.8 us; the launch traced here: 78.6 us
  Pallas kernels  73.6 us (93%)
  local copies, waits for them, and re-layouts  4.31 us (5%)
    pallas_call x1, Pallas kernels, main(): pl.pallas_call(main_kernel, out_shape=(jax.ShapeDtypeStruct((cols, rank),...  68.3 us
    pallas_call x1, Pallas kernels, finish(): pl.pallas_call(functools.partial(finish_kernel, scale), grid=(cols // wid...  5.35 us
    unnamed x10, local copies, waits for them, and re-layouts  4.31 us

profile of v3, /device:TPU:1, one launch (start us, length us, event | category | flops | bytes accessed | tf_op | source)
XLA Modules:
  0.0 78.6 jit_solution(6930547844997414358)
XLA Ops:
  0.6 0.0 copy-start
  0.6 68.3 %shard_map.58 = (bf16[2048,256]{1,0:T(8,128)(2,1)}, bf16[416,256]{1,0:T(8,128)(2,1)}, f32[8,256]{1,0:T(8,128)}) custom-call(bf16[416,2048]{1,0:T(8,128)(2,1)} %grad.1, f32[416,2048]{1,0:T(8,128)} %momentum.1, bf16[2048,256]{1,0:T(8,128)(2,1)} %basis_hbm.1), custom_call_target="tpu_custom_call" | custom-call | tf_op jit(solution)/shard_map/pallas_call | solution.py:337
  68.9 0.0 copy-done
  69.0 0.0 copy-start.1
  69.0 1.4 %copy-done.1 = bf16[416,2048]{1,0:T(8,128)(2,1)S(1)} copy-done((bf16[416,2048]{1,0:T(8,128)(2,1)S(1)}, bf16[416,2048]{1,0:T(8,128)(2,1)}, u32[]{:S(2)}) %copy-start.1) | copy-done | bytes 1703960
  70.4 0.0 copy-start.2
  70.4 1.2 %copy-done.2 = bf16[2048,256]{1,0:T(8,128)(2,1)S(1)} copy-done((bf16[2048,256]{1,0:T(8,128)(2,1)S(1)}, bf16[2048,256]{1,0:T(8,128)(2,1)}, u32[]{:S(2)}) %copy-start.2) | copy-done | bytes 1048600
  71.6 0.0 copy-start.3
  71.6 0.9 %copy-done.3 = bf16[416,256]{1,0:T(8,128)(2,1)S(1)} copy-done((bf16[416,256]{1,0:T(8,128)(2,1)S(1)}, bf16[416,256]{1,0:T(8,128)(2,1)}, u32[]{:S(2)}) %copy-start.3) | copy-done | bytes 213016
  72.6 0.0 copy-start.4
  72.6 0.7 copy-done.4
  73.3 5.4 %shard_map.59 = (f32[416,2048]{1,0:T(8,128)}, bf16[416,2048]{1,0:T(8,128)(2,1)}, bf16[2048,256]{1,0:T(8,128)(2,1)}) custom-call(bf16[416,2048]{1,0:T(8,128)(2,1)S(1)} %copy-done.1, f32[416,2048]{1,0:T(8,128)S(1)} %copy-done, bf16[416,256]{1,0:T(8,128)(2,1)S(1)} %copy-done.3, bf16[2048,256]{1,0:T(8,128)(2,1)S(1)} %copy-done.2, f32[8,256]{1,0:T(8,128)S(1)} %copy-done.4), custom_call_target="tpu_custom_call" | custom-call | tf_op jit(solution)/shard_map/pallas_call | solution.py:391
Async XLA Ops:
  0.6 68.3 %copy-start = (f32[416,2048]{1,0:T(8,128)S(1)}, f32[416,2048]{1,0:T(8,128)}, u32[]{:S(2)}) copy-start(f32[416,2048]{1,0:T(8,128)} %momentum.1) | copy-start | bytes 10223620
  69.0 1.5 %copy-start.1 = (bf16[416,2048]{1,0:T(8,128)(2,1)S(1)}, bf16[416,2048]{1,0:T(8,128)(2,1)}, u32[]{:S(2)}) copy-start(bf16[416,2048]{1,0:T(8,128)(2,1)} %grad.1) | copy-start | bytes 5111812
  70.4 1.2 %copy-start.2 = (bf16[2048,256]{1,0:T(8,128)(2,1)S(1)}, bf16[2048,256]{1,0:T(8,128)(2,1)}, u32[]{:S(2)}) copy-start(bf16[2048,256]{1,0:T(8,128)(2,1)} %get-tuple-element.7.rounded) | copy-start | bytes 3145732
  71.6 0.9 %copy-start.3 = (bf16[416,256]{1,0:T(8,128)(2,1)S(1)}, bf16[416,256]{1,0:T(8,128)(2,1)}, u32[]{:S(2)}) copy-start(bf16[416,256]{1,0:T(8,128)(2,1)} %get-tuple-element.6.ortho) | copy-start | bytes 638980
  72.6 0.7 copy-start.4

commit v4 on v3

--- a/solution.py
+++ b/solution.py
@@ -120,8 +120,8 @@
 
 def main_kernel(
     grad_hbm, momentum_hbm, basis_hbm,
-    rounded, ortho, scales,
-    grad_in, momentum_in, basis_in, high, low, piece, panel_got, panel,
+    new_momentum, rounded, ortho, scales,
+    grad_in, momentum_in, basis_in, high, low, high_turned, low_turned, piece, panel_got, panel,
     gram_own, gram_half, gram_got, gram_z, gram, inverse,
     cross, cross_got, lane_sent, lane_got, block, block_got, squares, halves,
     load_sem, ysend, yrecv, gsend, grecv, zgsend, zgrecv, g2send, g2recv, g3send, g3recv,
@@ -170,6 +170,10 @@
             greeted()
         if o:
             copies.append(send(piece.at[n, pl.ds(skip, fourth)], panel_got.at[o - 1], ysend.at[o - 1], yrecv.at[o - 1], tensor=p))
+    for n in range(8):
+        wide = slice(256 * n, 256 * n + 256)
+        high_turned[wide, :] = high[:, wide].T
+        low_turned[wide, :] = low[:, wide].T
     skip = pl.multiple_of(8 * (y % 2), 8)
     total = piece[3, pl.ds(skip, fourth), :]
     for copy in copies:
@@ -193,6 +197,23 @@
         ty, tx = (y + oy) % 4, (x + ox) % 4
         src = gram_half.at[pl.ds(pl.multiple_of((ty * 4 + tx) * 8, 8), 8)]
         spread.append(send(src, gram_got.at[n], gsend.at[n], grecv.at[n], fsdp=at(z, tx, core), tensor=ty))
+    for copy in gathers:
+        copy.wait_recv()
+    panel_high, panel_low = two_parts(panel[...])
+
+    def product(start):
+        upper = high_turned[pl.ds(pl.multiple_of(start, 256), 256), :]
+        lower = low_turned[pl.ds(pl.multiple_of(start, 256), 256), :]
+        return (
+            fast_dot(upper, panel_high, ((1,), (0,)))
+            + fast_dot(lower, panel_high, ((1,), (0,)))
+            + fast_dot(upper, panel_low, ((1,), (0,)))
+        )
+
+    crossing = []
+    for n, o in enumerate(ORDER):
+        cross[n] = product((1 - core) * 1024 + (x + o) % 4 * 256)
+        crossing.append(send(cross.at[n], cross_got.at[n], csend.at[n], crecv.at[n], fsdp=sibling))
     for copy in spread:
         copy.wait_recv()
     eight = (y * 4 + x) * 8
@@ -205,23 +226,6 @@
         for o in range(1, 8)
     ]
 
-    for copy in gathers:
-        copy.wait_recv()
-    panel_high, panel_low = two_parts(panel[...])
-
-    def product(start):
-        upper = high[:, pl.ds(pl.multiple_of(start, 256), 256)]
-        lower = low[:, pl.ds(pl.multiple_of(start, 256), 256)]
-        return (
-            fast_dot(upper, panel_high, ((0,), (0,)))
-            + fast_dot(lower, panel_high, ((0,), (0,)))
-            + fast_dot(upper, panel_low, ((0,), (0,)))
-        )
-
-    crossing = []
-    for n, o in enumerate(ORDER):
-        cross[n] = product((1 - core) * 1024 + (x + o) % 4 * 256)
-        crossing.append(send(cross.at[n], cross_got.at[n], csend.at[n], crecv.at[n], fsdp=sibling))
     passing = []
     for n, o in enumerate(ORDER):
         own = product(core * 1024 + (x + o) % 4 * 256)
@@ -295,6 +299,13 @@
     def block_of(o):
         return pl.ds(pl.multiple_of(core * 1024 + (x + 4 - o) % 4 * 256, 256), 256)
 
+    def block_there(o):
+        return pl.ds(pl.multiple_of((1 - core) * 1024 + (x + 4 - o) % 4 * 256, 256), 256)
+
+    def feed_back(span):
+        back = fast_dot(ortho[...], rounded[span, :], ((1,), (1,)))
+        new_momentum[:, span] = high[:, span].astype(F32) + low[:, span].astype(F32) - 0.05 * back
+
     across = [send(rounded.at[block_of(0)], rounded.at[block_of(0)], acsend.at[0], acrecv.at[0], fsdp=sibling)]
     total = jnp.zeros((8, rounded.shape[1]), F32)
     part = rounded[block_of(0), :].astype(F32)
@@ -307,6 +318,17 @@
         send(squares.at[slot], squares.at[slot], sqsend.at[n], sqrecv.at[n], fsdp=at(z, (x + ox) % 4, core), tensor=(y + oy) % 4)
         for n, (oy, ox) in enumerate(ALONG_YX)
     ]
+    feed_back(block_of(0))
+    across[0].wait_recv()
+    feed_back(block_there(0))
+    for n, o in enumerate((1, 3, 2)):
+        for copy in along_x[o]:
+            copy.wait_recv()
+        across.append(send(rounded.at[block_of(o)], rounded.at[block_of(o)], acsend.at[o], acrecv.at[o], fsdp=sibling))
+        feed_back(block_of(o))
+        if n < 2:
+            across[-1].wait_recv()
+            feed_back(block_there(o))
     for copy in spread:
         copy.wait_recv()
     total = squares[0]
@@ -314,15 +336,11 @@
         total = total + squares[n]
     halves[core] = total
     away = send(halves.at[core], halves.at[core], g3send.at[2], g3recv.at[2], fsdp=sibling)
-    for o in (1, 3, 2):
-        for copy in along_x[o]:
-            copy.wait_recv()
-        across.append(send(rounded.at[block_of(o)], rounded.at[block_of(o)], acsend.at[o], acrecv.at[o], fsdp=sibling))
+    across[-1].wait_recv()
+    feed_back(block_there(2))
     away.wait_recv()
     total = jnp.sum(halves[0] + halves[1], axis=0, keepdims=True)
     scales[...] = jnp.broadcast_to(lax.rsqrt(total + 1e-06), scales.shape)
-    for copy in across:
-        copy.wait_recv()
     for copy in sent:
         copy.wait_send()
 
@@ -337,18 +355,21 @@
     return pl.pallas_call(
         main_kernel,
         out_shape=(
+            jax.ShapeDtypeStruct((rows, cols), F32),
             jax.ShapeDtypeStruct((cols, rank), BF16),
             jax.ShapeDtypeStruct((rows, rank), BF16),
             jax.ShapeDtypeStruct((8, rank), F32),
         ),
         in_specs=[pl.BlockSpec(memory_space=pltpu.HBM)] * 3,
-        out_specs=(pl.BlockSpec(memory_space=pltpu.VMEM),) * 3,
+        out_specs=(pl.BlockSpec(memory_space=pltpu.VMEM),) * 4,
         scratch_shapes=[
             vmem((4, fourth + 8, cols), BF16),
             vmem((4, fourth + 8, cols), F32),
             vmem((cols, rank), BF16),
             vmem((rows, cols), BF16),
             vmem((rows, cols), BF16),
+            vmem((cols, rows), BF16),
+            vmem((cols, rows), BF16),
             vmem((4, fourth + 8, rank), F32),
             vmem((3, fourth, rank), F32),
             vmem((rows, rank), F32),
@@ -369,46 +390,53 @@
             dma((9,)),
             *[dma(shape) for shape in pairs for _ in range(2)],
         ],
-        compiler_params=pltpu.CompilerParams(collective_id=0, has_side_effects=True, vmem_limit_bytes=60 << 20),
-    )(grad, momentum, basis)
-
-
-def finish_kernel(scale, grad, momentum, ortho, rounded, scales, new_momentum, update, basis_next):
-    columns = rounded[...]
-    following = (columns.astype(F32) * scales[:1, :]).astype(BF16)
-    basis_next[...] = following
-    blended = momentum[...] + grad[...].astype(F32)
-    new_momentum[...] = blended - 0.05 * fast_dot(ortho[...], columns, ((1,), (1,)))
-    update[...] = (scale * fast_dot(ortho[...], following, ((1,), (1,)))).astype(BF16)
-
-
-def finish(scale, grad, momentum, ortho, rounded, scales):
-    rows, cols = grad.shape
+        compiler_params=pltpu.CompilerParams(collective_id=0, has_side_effects=True, vmem_limit_bytes=40 << 20),
+    )(*[pltpu.with_memory_space_constraint(v, pltpu.HBM) for v in (grad, momentum, basis)])
+
+
+def finish_kernel(scale, momentum, rounded, ortho, scales, new_momentum, update, basis_next, part, following, sems):
+    copies = [pltpu.make_async_copy(momentum, new_momentum, sems.at[0])]
+    copies[0].start()
+    wide = 512
+    for n in range(rounded.shape[0] // wide):
+        span = pl.ds(n * wide, wide)
+        block = (rounded[span, :].astype(F32) * scales[:1, :]).astype(BF16)
+        following[span, :] = block
+        part[n] = (scale * fast_dot(ortho[...], block, ((1,), (1,)))).astype(BF16)
+        copies.append(pltpu.make_async_copy(following.at[span], basis_next.at[span], sems.at[2 * n + 1]))
+        copies.append(pltpu.make_async_copy(part.at[n], update.at[:, span], sems.at[2 * n + 2]))
+        copies[-2].start()
+        copies[-1].start()
+    for copy in copies:
+        copy.wait()
+
+
+def finish(scale, momentum, rounded, ortho, scales):
+    rows, cols = momentum.shape
     rank = ortho.shape[1]
-    wide = 256
-    part = pl.BlockSpec((rows, wide), lambda i: (0, i))
-    tall = pl.BlockSpec((wide, rank), lambda i: (i, 0))
     return pl.pallas_call(
         functools.partial(finish_kernel, scale),
-        grid=(cols // wide,),
         out_shape=(
             jax.ShapeDtypeStruct((rows, cols), F32),
             jax.ShapeDtypeStruct((rows, cols), BF16),
             jax.ShapeDtypeStruct((cols, rank), BF16),
         ),
-        in_specs=[
-            part, part, pl.BlockSpec((rows, rank), lambda i: (0, 0)), tall, pl.BlockSpec((8, rank), lambda i: (0, 0)),
+        in_specs=[pl.BlockSpec(memory_space=pl.ANY)] + [pl.BlockSpec(memory_space=pltpu.VMEM)] * 3,
+        out_specs=(pl.BlockSpec(memory_space=pl.ANY),) * 3,
+        scratch_shapes=[
+            pltpu.VMEM((cols // 512, rows, 512), BF16),
+            pltpu.VMEM((cols, rank), BF16),
+            pltpu.SemaphoreType.DMA((2 * cols // 512 + 1,)),
         ],
-        out_specs=(part, part, tall),
-        compiler_params=pltpu.CompilerParams(vmem_limit_bytes=32 << 20),
-    )(grad, momentum, ortho, rounded, scales)
+        compiler_params=pltpu.CompilerParams(vmem_limit_bytes=16 << 20),
+    )(momentum, rounded, ortho, scales)
 
 
 def on_device(grad, momentum, basis):
     rows_here, cols_here = grad.shape
     scale = math.sqrt(rows_here * lax.axis_size("fsdp") * cols_here * lax.axis_size("tensor") / basis.shape[1])
-    rounded, ortho, scales = main(grad, momentum, basis)
-    return finish(scale, grad, momentum, ortho, rounded, scales)
+    momentum, rounded, ortho, scales = main(grad, momentum, basis)
+    return finish(scale, momentum, rounded, ortho, scales)
 
 
 def solution(mesh):

time: 78.8 us -> 71 us (0.901)
  local copies, waits for them, and re-layouts: 4.31 us -> 0 us
  Pallas kernels: 73.6 us -> 70.2 us
    unnamed x10 -> x0, local copies, waits for them, and re-layouts: 4.31 us -> none
    pallas_call x2, Pallas kernels: 73.6 us -> 70.2 us  [the longest x1 67.5 us: main(): pl.pallas_call(main_kernel, out_shape=(jax.ShapeDtypeStruct((rows, cols),...]
where the time goes in v4:
time: 71 us
  Pallas kernels  70.2 us (99%)
  between operations  0.8 us (1%)
    pallas_call x1, Pallas kernels, main(): pl.pallas_call(main_kernel, out_shape=(jax.ShapeDtypeStruct((rows, cols),...  67.5 us
    pallas_call x1, Pallas kernels, finish(): pl.pallas_call(functools.partial(finish_kernel, scale), out_shape=(jax.Sh...  2.69 us

profile of v4, /device:TPU:1, one launch (start us, length us, event | category | flops | bytes accessed | tf_op | source)
XLA Modules:
  0.0 71.0 jit_solution(7549095078837271777)
XLA Ops:
  0.6 67.5 %shard_map.58 = (f32[416,2048]{1,0:T(8,128)S(1)}, bf16[2048,256]{1,0:T(8,128)(2,1)S(1)}, bf16[416,256]{1,0:T(8,128)(2,1)S(1)}, f32[8,256]{1,0:T(8,128)S(1)}) custom-call(bf16[416,2048]{1,0:T(8,128)(2,1)} %grad_hbm.1, f32[416,2048]{1,0:T(8,128)} %momentum_hbm.1, bf16[2048,256]{1,0:T(8,128)(2,1)} %basis_hbm.1), custom_call_target="tpu_custom_call" | custom-call | tf_op jit(solution)/shard_map/pallas_call | solution.py:355
  68.1 2.7 %shard_map.59 = (f32[416,2048]{1,0:T(8,128)}, bf16[416,2048]{1,0:T(8,128)(2,1)}, bf16[2048,256]{1,0:T(8,128)(2,1)}) custom-call(f32[416,2048]{1,0:T(8,128)S(1)} %get-tuple-element.7.momentum, bf16[2048,256]{1,0:T(8,128)(2,1)S(1)} %get-tuple-element.8.rounded, bf16[416,256]{1,0:T(8,128)(2,1)S(1)} %get-tuple-element.9.ortho, f32[8,256]{1,0:T(8,128)S(1)} %get-tuple-element.10.scales), custom_call_target="tpu_custom_call" | custom-call | tf_op jit(solution)/shard_map/pallas_call | solution.py:417

commit v5 on v4

--- a/solution.py
+++ b/solution.py
@@ -120,12 +120,12 @@
 
 def main_kernel(
     grad_hbm, momentum_hbm, basis_hbm,
-    new_momentum, rounded, ortho, scales,
-    grad_in, momentum_in, basis_in, high, low, high_turned, low_turned, piece, panel_got, panel,
+    new_momentum, rounded, ortho, ortho_low, scales,
+    grad_in, momentum_in, basis_in, high, low, high_turned, low_turned, piece, piece_sent, panel_got, panel, panel_own, panel_there,
     gram_own, gram_half, gram_got, gram_z, gram, inverse,
-    cross, cross_got, lane_sent, lane_got, block, block_got, squares, halves,
+    cross, cross_got, lane_sent, lane_got, block, block_got, squares, squares_z, halves,
     load_sem, ysend, yrecv, gsend, grecv, zgsend, zgrecv, g2send, g2recv, g3send, g3recv,
-    csend, crecv, xsend, xrecv, zsend, zrecv, azsend, azrecv, axsend, axrecv, acsend, acrecv, sqsend, sqrecv,
+    csend, crecv, xsend, xrecv, zsend, zrecv, azsend, azrecv, axsend, axrecv, acsend, acrecv, sqsend, sqrecv, sqzsend, sqzrecv,
 ):
     z, x, core, y = place()
     rows = grad_hbm.shape[0]
@@ -169,7 +169,8 @@
         if n == 0:
             greeted()
         if o:
-            copies.append(send(piece.at[n, pl.ds(skip, fourth)], panel_got.at[o - 1], ysend.at[o - 1], yrecv.at[o - 1], tensor=p))
+            piece_sent[n] = piece[n, pl.ds(skip, fourth), :].astype(BF16)
+            copies.append(send(piece_sent.at[n], panel_got.at[o - 1], ysend.at[o - 1], yrecv.at[o - 1], tensor=p))
     for n in range(8):
         wide = slice(256 * n, 256 * n + 256)
         high_turned[wide, :] = high[:, wide].T
@@ -179,15 +180,17 @@
     for copy in copies:
         copy.wait_recv()
     for o in (1, 2, 3):
-        total = total + panel_got[o - 1]
+        total = total + panel_got[o - 1].astype(F32)
     mine = pl.ds(pl.multiple_of(y * fourth, 8), fourth)
+    panel_own[...] = total.astype(BF16)
+    gathers = [
+        send(panel_own, panel_there.at[o - 1], ysend.at[2 + o], yrecv.at[2 + o], tensor=(y + o) % 4) for o in (1, 2, 3)
+    ]
+
+    half = 128
+    total = panel_own[...].astype(F32)
     panel[mine, :] = total
-    gathers = [
-        send(panel.at[mine], panel.at[mine], ysend.at[2 + o], yrecv.at[2 + o], tensor=(y + o) % 4) for o in (1, 2, 3)
-    ]
-
-    half = 128
-    gram_own[...] = dot(total, total, ((0,), (0,)))
+    gram_own[...] = fast_dot(panel_own[...], panel_own[...], ((0,), (0,)))
     away = send(gram_own.at[pl.ds(pl.multiple_of((1 - core) * half, half), half)], gram_half, g3send.at[0], g3recv.at[0], fsdp=sibling)
     away.wait_recv()
     kept = pl.ds(pl.multiple_of(core * half, half), half)
@@ -199,7 +202,9 @@
         spread.append(send(src, gram_got.at[n], gsend.at[n], grecv.at[n], fsdp=at(z, tx, core), tensor=ty))
     for copy in gathers:
         copy.wait_recv()
-    panel_high, panel_low = two_parts(panel[...])
+    for o in (1, 2, 3):
+        panel[pl.ds(pl.multiple_of((y + 4 - o) % 4 * fourth, 8), fourth), :] = panel_there[o - 1].astype(F32)
+    panel_high = panel[...].astype(BF16)
 
     def product(start):
         upper = high_turned[pl.ds(pl.multiple_of(start, 256), 256), :]
@@ -207,7 +212,6 @@
         return (
             fast_dot(upper, panel_high, ((1,), (0,)))
             + fast_dot(lower, panel_high, ((1,), (0,)))
-            + fast_dot(upper, panel_low, ((1,), (0,)))
         )
 
     crossing = []
@@ -276,7 +280,8 @@
         return pl.ds(pl.multiple_of(core * 1024 + x * 256 + z_of * 32, 32), 32)
 
     here = rows_of(z)
-    rounded[here, :] = dot(total, inverse[...], ((1,), (1,))).astype(BF16)
+    own = dot(total, inverse[...], ((1,), (1,))).astype(BF16)
+    rounded[here, :] = own
     along_z = [
         send(rounded.at[here], rounded.at[here], azsend.at[o - 1], azrecv.at[o - 1], fsdp=at((z + o) % 8, x, core))
         for o in range(1, 8)
@@ -291,10 +296,31 @@
             )
 
     pass_on(0)
-    ortho[...] = dot(panel[...], inverse[...], ((1,), (1,))).astype(BF16)
-    for zo in (1, 7, 2, 6, 3, 5, 4):
+    own = own.astype(F32)
+    slot = y * 4 + x
+    squares[slot] = jnp.sum(own * own, axis=0, keepdims=True)
+    spread = [
+        send(squares.at[slot], squares.at[slot], sqsend.at[n], sqrecv.at[n], fsdp=at(z, (x + ox) % 4, core), tensor=(y + oy) % 4)
+        for n, (oy, ox) in enumerate(ALONG_YX)
+    ]
+    upper, lower = two_parts(dot(panel[...], inverse[...], ((1,), (1,))))
+    ortho[...] = upper
+    ortho_low[...] = lower
+    for zo in (1, 7, 2, 6, 3, 5):
         along_z[zo - 1].wait_recv()
         pass_on(zo)
+    for copy in spread:
+        copy.wait_recv()
+    total = squares[0]
+    for n in range(1, 16):
+        total = total + squares[n]
+    squares_z[z] = total
+    around = [
+        send(squares_z.at[z], squares_z.at[z], sqzsend.at[o - 1], sqzrecv.at[o - 1], fsdp=at((z + o) % 8, x, core))
+        for o in range(1, 8)
+    ]
+    along_z[3].wait_recv()
+    pass_on(4)
 
     def block_of(o):
         return pl.ds(pl.multiple_of(core * 1024 + (x + 4 - o) % 4 * 256, 256), 256)
@@ -307,17 +333,6 @@
         new_momentum[:, span] = high[:, span].astype(F32) + low[:, span].astype(F32) - 0.05 * back
 
     across = [send(rounded.at[block_of(0)], rounded.at[block_of(0)], acsend.at[0], acrecv.at[0], fsdp=sibling)]
-    total = jnp.zeros((8, rounded.shape[1]), F32)
-    part = rounded[block_of(0), :].astype(F32)
-    part = part * part
-    for i in range(32):
-        total = total + part[8 * i : 8 * i + 8, :]
-    slot = y * 4 + x
-    squares[slot] = total
-    spread = [
-        send(squares.at[slot], squares.at[slot], sqsend.at[n], sqrecv.at[n], fsdp=at(z, (x + ox) % 4, core), tensor=(y + oy) % 4)
-        for n, (oy, ox) in enumerate(ALONG_YX)
-    ]
     feed_back(block_of(0))
     across[0].wait_recv()
     feed_back(block_there(0))
@@ -329,17 +344,17 @@
         if n < 2:
             across[-1].wait_recv()
             feed_back(block_there(o))
-    for copy in spread:
-        copy.wait_recv()
-    total = squares[0]
-    for n in range(1, 16):
-        total = total + squares[n]
+    for copy in around:
+        copy.wait_recv()
+    total = squares_z[0]
+    for n in range(1, 8):
+        total = total + squares_z[n]
     halves[core] = total
     away = send(halves.at[core], halves.at[core], g3send.at[2], g3recv.at[2], fsdp=sibling)
     across[-1].wait_recv()
     feed_back(block_there(2))
     away.wait_recv()
-    total = jnp.sum(halves[0] + halves[1], axis=0, keepdims=True)
+    total = halves[0] + halves[1]
     scales[...] = jnp.broadcast_to(lax.rsqrt(total + 1e-06), scales.shape)
     for copy in sent:
         copy.wait_send()
@@ -351,17 +366,18 @@
     fourth = rows // 4
     dma = pltpu.SemaphoreType.DMA
     vmem = pltpu.VMEM
-    pairs = ((6,), (15,), (7,), (15,), (3,), (4,), (3,), (7,), (7,), (3, 8), (4,), (15,))
+    pairs = ((6,), (15,), (7,), (15,), (3,), (4,), (3,), (7,), (7,), (3, 8), (4,), (15,), (7,))
     return pl.pallas_call(
         main_kernel,
         out_shape=(
             jax.ShapeDtypeStruct((rows, cols), F32),
             jax.ShapeDtypeStruct((cols, rank), BF16),
             jax.ShapeDtypeStruct((rows, rank), BF16),
+            jax.ShapeDtypeStruct((rows, rank), BF16),
             jax.ShapeDtypeStruct((8, rank), F32),
         ),
         in_specs=[pl.BlockSpec(memory_space=pltpu.HBM)] * 3,
-        out_specs=(pl.BlockSpec(memory_space=pltpu.VMEM),) * 4,
+        out_specs=(pl.BlockSpec(memory_space=pltpu.VMEM),) * 5,
         scratch_shapes=[
             vmem((4, fourth + 8, cols), BF16),
             vmem((4, fourth + 8, cols), F32),
@@ -371,8 +387,11 @@
             vmem((cols, rows), BF16),
             vmem((cols, rows), BF16),
             vmem((4, fourth + 8, rank), F32),
-            vmem((3, fourth, rank), F32),
+            vmem((3, fourth, rank), BF16),
+            vmem((3, fourth, rank), BF16),
             vmem((rows, rank), F32),
+            vmem((fourth, rank), BF16),
+            vmem((3, fourth, rank), BF16),
             vmem((rank, rank), F32),
             vmem((rank // 2, rank), F32),
             vmem((15, 8, rank), F32),
@@ -385,8 +404,9 @@
             vmem((3, 256, rank), BF16),
             vmem((256, rank), F32),
             vmem((7, 32, rank), F32),
-            vmem((16, 8, rank), F32),
-            vmem((2, 8, rank), F32),
+            vmem((16, 1, rank), F32),
+            vmem((8, 1, rank), F32),
+            vmem((2, 1, rank), F32),
             dma((9,)),
             *[dma(shape) for shape in pairs for _ in range(2)],
         ],
@@ -394,7 +414,7 @@
     )(*[pltpu.with_memory_space_constraint(v, pltpu.HBM) for v in (grad, momentum, basis)])
 
 
-def finish_kernel(scale, momentum, rounded, ortho, scales, new_momentum, update, basis_next, part, following, sems):
+def finish_kernel(scale, momentum, rounded, ortho, ortho_low, scales, new_momentum, update, basis_next, part, following, sems):
     copies = [pltpu.make_async_copy(momentum, new_momentum, sems.at[0])]
     copies[0].start()
     wide = 512
@@ -402,7 +422,8 @@
         span = pl.ds(n * wide, wide)
         block = (rounded[span, :].astype(F32) * scales[:1, :]).astype(BF16)
         following[span, :] = block
-        part[n] = (scale * fast_dot(ortho[...], block, ((1,), (1,)))).astype(BF16)
+        step = fast_dot(ortho[...], block, ((1,), (1,))) + fast_dot(ortho_low[...], block, ((1,), (1,)))
+        part[n] = (scale * step).astype(BF16)
         copies.append(pltpu.make_async_copy(following.at[span], basis_next.at[span], sems.at[2 * n + 1]))
         copies.append(pltpu.make_async_copy(part.at[n], update.at[:, span], sems.at[2 * n + 2]))
         copies[-2].start()
@@ -411,7 +432,7 @@
         copy.wait()
 
 
-def finish(scale, momentum, rounded, ortho, scales):
+def finish(scale, momentum, rounded, ortho, ortho_low, scales):
     rows, cols = momentum.shape
     rank = ortho.shape[1]
     return pl.pallas_call(
@@ -421,7 +442,7 @@
             jax.ShapeDtypeStruct((rows, cols), BF16),
             jax.ShapeDtypeStruct((cols, rank), BF16),
         ),
-        in_specs=[pl.BlockSpec(memory_space=pl.ANY)] + [pl.BlockSpec(memory_space=pltpu.VMEM)] * 3,
+        in_specs=[pl.BlockSpec(memory_space=pl.ANY)] + [pl.BlockSpec(memory_space=pltpu.VMEM)] * 4,
         out_specs=(pl.BlockSpec(memory_space=pl.ANY),) * 3,
         scratch_shapes=[
             pltpu.VMEM((cols // 512, rows, 512), BF16),
@@ -429,14 +450,14 @@
             pltpu.SemaphoreType.DMA((2 * cols // 512 + 1,)),
         ],
         compiler_params=pltpu.CompilerParams(vmem_limit_bytes=16 << 20),
-    )(momentum, rounded, ortho, scales)
+    )(momentum, rounded, ortho, ortho_low, scales)
 
 
 def on_device(grad, momentum, basis):
     rows_here, cols_here = grad.shape
     scale = math.sqrt(rows_here * lax.axis_size("fsdp") * cols_here * lax.axis_size("tensor") / basis.shape[1])
-    momentum, rounded, ortho, scales = main(grad, momentum, basis)
-    return finish(scale, momentum, rounded, ortho, scales)
+    momentum, *rest = main(grad, momentum, basis)
+    return finish(scale, momentum, *rest)
 
 
 def solution(mesh):

time: 71 us -> 65.3 us (0.920)
  Pallas kernels: 70.2 us -> 64.4 us
    pallas_call x1, Pallas kernels: 67.5 us -> 61.7 us  [main(): pl.pallas_call(main_kernel, out_shape=(jax.ShapeDtypeStruct((rows, cols),...]
where the time goes in v5:
time: 65.3 us; the launch traced here: 65.2 us
  Pallas kernels  64.4 us (99%)
  between operations  0.8 us (1%)
    pallas_call x1, Pallas kernels, main(): pl.pallas_call(main_kernel, out_shape=(jax.ShapeDtypeStruct((rows, cols),...  61.7 us
    pallas_call x1, Pallas kernels, finish(): pl.pallas_call(functools.partial(finish_kernel, scale), out_shape=(jax.Sh...  2.69 us

profile of v5, /device:TPU:1, one launch (start us, length us, event | category | flops | bytes accessed | tf_op | source)
XLA Modules:
  0.0 65.2 jit_solution(17025332828300016777)
XLA Ops:
  0.6 61.7 %shard_map.58 = (f32[416,2048]{1,0:T(8,128)S(1)}, bf16[2048,256]{1,0:T(8,128)(2,1)S(1)}, bf16[416,256]{1,0:T(8,128)(2,1)S(1)}, bf16[416,256]{1,0:T(8,128)(2,1)S(1)}, f32[8,256]{1,0:T(8,128)S(1)}) custom-call(bf16[416,2048]{1,0:T(8,128)(2,1)} %grad_hbm.1, f32[416,2048]{1,0:T(8,128)} %momentum_hbm.1, bf16[2048,256]{1,0:T(8,128)(2,1)} %basis_hbm.1), custom_call_target="tpu_custom_call" | custom-call | tf_op jit(solution)/shard_map/pallas_call | solution.py:370
  62.3 2.7 %shard_map.59 = (f32[416,2048]{1,0:T(8,128)}, bf16[416,2048]{1,0:T(8,128)(2,1)}, bf16[2048,256]{1,0:T(8,128)(2,1)}) custom-call(f32[416,2048]{1,0:T(8,128)S(1)} %get-tuple-element.8.momentum, bf16[2048,256]{1,0:T(8,128)(2,1)S(1)} %get-tuple-element.9.rounded, bf16[416,256]{1,0:T(8,128)(2,1)S(1)} %get-tuple-element.10.ortho, ...), custom_call_target="tpu_custom_call" | custom-call | tf_op jit(solution)/shard_map/pallas_call | solution.py:438

commit v6 on v5

--- a/solution.py
+++ b/solution.py
@@ -115,7 +115,13 @@
 
 
 ORDER = (2, 1, 3, 0)
-ALONG_YX = tuple((oy, ox) for oy in range(4) for ox in range(4) if oy or ox)
+ALONG_YX = tuple(
+    sorted(
+        ((oy, ox) for oy in range(4) for ox in range(4) if oy or ox),
+        key=lambda o: -min(o[0], 4 - o[0]) - min(o[1], 4 - o[1]),
+    )
+)
+ALONG_Z = (4, 3, 5, 2, 6, 1, 7)
 
 
 def main_kernel(
@@ -132,8 +138,9 @@
     fourth = rows // 4
     taller = fourth + 8
     sibling = at(z, x, 1 - core)
-    others = [{"fsdp": at((z + o) % 8, x, core)} for o in range(1, 8)]
-    others += [{"fsdp": at(z, (x + ox) % 4, core), "tensor": (y + oy) % 4} for oy, ox in ALONG_YX]
+    across_z = [{"fsdp": at((z + o) % 8, x, core)} for o in ALONG_Z]
+    others = across_z + [{"tensor": (y + o) % 4} for o in (2, 1, 3)]
+    others += [{"fsdp": at(z, (x + o) % 4, core)} for o in (2, 1, 3)]
     others += [{"fsdp": sibling}]
     greeted = greet(others)
     basis_load = pltpu.make_async_copy(basis_hbm, basis_in, load_sem.at[8])
@@ -218,20 +225,8 @@
     for n, o in enumerate(ORDER):
         cross[n] = product((1 - core) * 1024 + (x + o) % 4 * 256)
         crossing.append(send(cross.at[n], cross_got.at[n], csend.at[n], crecv.at[n], fsdp=sibling))
-    for copy in spread:
-        copy.wait_recv()
-    eight = (y * 4 + x) * 8
-    total = gram_half[pl.ds(pl.multiple_of(eight, 8), 8), :]
-    for n in range(15):
-        total = total + gram_got[n]
-    gram_z[z] = total
-    around = [
-        send(gram_z.at[z], gram_z.at[z], zgsend.at[o - 1], zgrecv.at[o - 1], fsdp=at((z + o) % 8, x, core))
-        for o in range(1, 8)
-    ]
-
     passing = []
-    for n, o in enumerate(ORDER):
+    for n, o in ((0, 2), (1, 1)):
         own = product(core * 1024 + (x + o) % 4 * 256)
         crossing[n].wait_recv()
         own = own + cross_got[n]
@@ -242,6 +237,28 @@
             )
         else:
             block[...] = own
+    for copy in spread:
+        copy.wait_recv()
+    eight = (y * 4 + x) * 8
+    total = gram_half[pl.ds(pl.multiple_of(eight, 8), 8), :]
+    for n in range(15):
+        total = total + gram_got[n]
+    gram_z[z] = total
+    around = [
+        send(gram_z.at[z], gram_z.at[z], zgsend.at[o - 1], zgrecv.at[o - 1], fsdp=at((z + o) % 8, x, core))
+        for o in ALONG_Z
+    ]
+    for n, o in ((2, 3), (3, 0)):
+        own = product(core * 1024 + (x + o) % 4 * 256)
+        crossing[n].wait_recv()
+        own = own + cross_got[n]
+        if o:
+            lane_sent[n] = own.astype(BF16)
+            passing.append(
+                send(lane_sent.at[n], lane_got.at[o - 1], xsend.at[o - 1], xrecv.at[o - 1], fsdp=at(z, (x + o) % 4, core))
+            )
+        else:
+            block[...] = own
 
     for copy in around:
         copy.wait_recv()
@@ -262,7 +279,7 @@
         copy.wait_recv()
     block[...] = block[...] + lane_got[0].astype(F32) + lane_got[1].astype(F32) + lane_got[2].astype(F32)
     last = []
-    for o in range(1, 8):
+    for o in ALONG_Z:
         to = (z + o) % 8
         last.append(
             send(block.at[pl.ds(pl.multiple_of(to * 32, 32), 32)], block_got.at[o - 1], zsend.at[o - 1], zrecv.at[o - 1],
@@ -317,7 +334,7 @@
     squares_z[z] = total
     around = [
         send(squares_z.at[z], squares_z.at[z], sqzsend.at[o - 1], sqzrecv.at[o - 1], fsdp=at((z + o) % 8, x, core))
-        for o in range(1, 8)
+        for o in ALONG_Z
     ]
     along_z[3].wait_recv()
     pass_on(4)
@@ -415,17 +432,22 @@
 
 
 def finish_kernel(scale, momentum, rounded, ortho, ortho_low, scales, new_momentum, update, basis_next, part, following, sems):
-    copies = [pltpu.make_async_copy(momentum, new_momentum, sems.at[0])]
-    copies[0].start()
     wide = 512
-    for n in range(rounded.shape[0] // wide):
+    many = rounded.shape[0] // wide
+    tall = momentum.shape[0] // many
+    copies = []
+    for n in range(many):
+        span = pl.ds(n * tall, tall)
+        copies.append(pltpu.make_async_copy(momentum.at[span], new_momentum.at[span], sems.at[2 * many + n]))
+        copies[-1].start()
+    for n in range(many):
         span = pl.ds(n * wide, wide)
         block = (rounded[span, :].astype(F32) * scales[:1, :]).astype(BF16)
         following[span, :] = block
         step = fast_dot(ortho[...], block, ((1,), (1,))) + fast_dot(ortho_low[...], block, ((1,), (1,)))
         part[n] = (scale * step).astype(BF16)
-        copies.append(pltpu.make_async_copy(following.at[span], basis_next.at[span], sems.at[2 * n + 1]))
-        copies.append(pltpu.make_async_copy(part.at[n], update.at[:, span], sems.at[2 * n + 2]))
+        copies.append(pltpu.make_async_copy(following.at[span], basis_next.at[span], sems.at[2 * n]))
+        copies.append(pltpu.make_async_copy(part.at[n], update.at[:, span], sems.at[2 * n + 1]))
         copies[-2].start()
         copies[-1].start()
     for copy in copies:
@@ -447,7 +469,7 @@
         scratch_shapes=[
             pltpu.VMEM((cols // 512, rows, 512), BF16),
             pltpu.VMEM((cols, rank), BF16),
-            pltpu.SemaphoreType.DMA((2 * cols // 512 + 1,)),
+            pltpu.SemaphoreType.DMA((3 * cols // 512,)),
         ],
         compiler_params=pltpu.CompilerParams(vmem_limit_bytes=16 << 20),
     )(momentum, rounded, ortho, ortho_low, scales)

time: 65.3 us -> 64 us (0.980)
  Pallas kernels: 64.4 us -> 63 us
    pallas_call x1, Pallas kernels: 61.7 us -> 60.3 us  [main(): pl.pallas_call(main_kernel, out_shape=(jax.ShapeDtypeStruct((rows, cols),...]
where the time goes in v6:
time: 64 us; the launch traced here: 63.8 us
  Pallas kernels  63 us (98%)
  between operations  0.8 us (1%)
    pallas_call x1, Pallas kernels, main(): pl.pallas_call(main_kernel, out_shape=(jax.ShapeDtypeStruct((rows, cols),...  60.3 us
    pallas_call x1, Pallas kernels, finish(): pl.pallas_call(functools.partial(finish_kernel, scale), out_shape=(jax.Sh...  2.71 us

profile of v6, /device:TPU:1, one launch (start us, length us, event | category | flops | bytes accessed | tf_op | source)
XLA Modules:
  0.0 63.8 jit_solution(3027391503554473143)
XLA Ops:
  0.6 60.3 %shard_map.58 = (f32[416,2048]{1,0:T(8,128)S(1)}, bf16[2048,256]{1,0:T(8,128)(2,1)S(1)}, bf16[416,256]{1,0:T(8,128)(2,1)S(1)}, bf16[416,256]{1,0:T(8,128)(2,1)S(1)}, f32[8,256]{1,0:T(8,128)S(1)}) custom-call(bf16[416,2048]{1,0:T(8,128)(2,1)} %grad_hbm.1, f32[416,2048]{1,0:T(8,128)} %momentum_hbm.1, bf16[2048,256]{1,0:T(8,128)(2,1)} %basis_hbm.1), custom_call_target="tpu_custom_call" | custom-call | tf_op jit(solution)/shard_map/pallas_call | solution.py:387
  61.0 2.7 %shard_map.59 = (f32[416,2048]{1,0:T(8,128)}, bf16[416,2048]{1,0:T(8,128)(2,1)}, bf16[2048,256]{1,0:T(8,128)(2,1)}) custom-call(f32[416,2048]{1,0:T(8,128)S(1)} %get-tuple-element.8.momentum, bf16[2048,256]{1,0:T(8,128)(2,1)S(1)} %get-tuple-element.9.rounded, bf16[416,256]{1,0:T(8,128)(2,1)S(1)} %get-tuple-element.10.ortho, ...), custom_call_target="tpu_custom_call" | custom-call | tf_op jit(solution)/shard_map/pallas_call | solution.py:460

commit v7 on v6

--- a/solution.py
+++ b/solution.py
@@ -176,27 +176,26 @@
         if n == 0:
             greeted()
         if o:
-            piece_sent[n] = piece[n, pl.ds(skip, fourth), :].astype(BF16)
+            piece_sent[n] = piece[n].astype(BF16)
             copies.append(send(piece_sent.at[n], panel_got.at[o - 1], ysend.at[o - 1], yrecv.at[o - 1], tensor=p))
     for n in range(8):
         wide = slice(256 * n, 256 * n + 256)
         high_turned[wide, :] = high[:, wide].T
         low_turned[wide, :] = low[:, wide].T
     skip = pl.multiple_of(8 * (y % 2), 8)
+    for copy in copies:
+        copy.wait_recv()
+    for o in (1, 2, 3):
+        piece[3] = piece[3] + panel_got[o - 1].astype(F32)
     total = piece[3, pl.ds(skip, fourth), :]
-    for copy in copies:
-        copy.wait_recv()
-    for o in (1, 2, 3):
-        total = total + panel_got[o - 1].astype(F32)
     mine = pl.ds(pl.multiple_of(y * fourth, 8), fourth)
-    panel_own[...] = total.astype(BF16)
+    panel_own[...] = jnp.concatenate([total, jnp.zeros((8, total.shape[1]), F32)], 0).astype(BF16)
     gathers = [
         send(panel_own, panel_there.at[o - 1], ysend.at[2 + o], yrecv.at[2 + o], tensor=(y + o) % 4) for o in (1, 2, 3)
     ]
 
     half = 128
-    total = panel_own[...].astype(F32)
-    panel[mine, :] = total
+    panel[mine, :] = panel_own[...].astype(F32)[:fourth]
     gram_own[...] = fast_dot(panel_own[...], panel_own[...], ((0,), (0,)))
     away = send(gram_own.at[pl.ds(pl.multiple_of((1 - core) * half, half), half)], gram_half, g3send.at[0], g3recv.at[0], fsdp=sibling)
     away.wait_recv()
@@ -210,7 +209,7 @@
     for copy in gathers:
         copy.wait_recv()
     for o in (1, 2, 3):
-        panel[pl.ds(pl.multiple_of((y + 4 - o) % 4 * fourth, 8), fourth), :] = panel_there[o - 1].astype(F32)
+        panel[pl.ds(pl.multiple_of((y + 4 - o) % 4 * fourth, 8), fourth), :] = panel_there[o - 1].astype(F32)[:fourth]
     panel_high = panel[...].astype(BF16)
 
     def product(start):
@@ -404,11 +403,11 @@
             vmem((cols, rows), BF16),
             vmem((cols, rows), BF16),
             vmem((4, fourth + 8, rank), F32),
-            vmem((3, fourth, rank), BF16),
-            vmem((3, fourth, rank), BF16),
+            vmem((3, fourth + 8, rank), BF16),
+            vmem((3, fourth + 8, rank), BF16),
             vmem((rows, rank), F32),
-            vmem((fourth, rank), BF16),
-            vmem((3, fourth, rank), BF16),
+            vmem((fourth + 8, rank), BF16),
+            vmem((3, fourth + 8, rank), BF16),
             vmem((rank, rank), F32),
             vmem((rank // 2, rank), F32),
             vmem((15, 8, rank), F32),

time: 64 us -> 64.2 us (level)
  no operation moved by 1% of the time
where the time goes in v7:
time: 64.2 us; the launch traced here: 63.7 us
  Pallas kernels  62.9 us (98%)
  between operations  0.8 us (1%)
    pallas_call x1, Pallas kernels, main(): pl.pallas_call(main_kernel, out_shape=(jax.ShapeDtypeStruct((rows, cols),...  60.2 us
    pallas_call x1, Pallas kernels, finish(): pl.pallas_call(functools.partial(finish_kernel, scale), out_shape=(jax.Sh...  2.71 us

profile of v7, /device:TPU:1, one launch (start us, length us, event | category | flops | bytes accessed | tf_op | source)
XLA Modules:
  0.0 63.7 jit_solution(15047011492940906179)
XLA Ops:
  0.6 60.2 %shard_map.58 = (f32[416,2048]{1,0:T(8,128)S(1)}, bf16[2048,256]{1,0:T(8,128)(2,1)S(1)}, bf16[416,256]{1,0:T(8,128)(2,1)S(1)}, bf16[416,256]{1,0:T(8,128)(2,1)S(1)}, f32[8,256]{1,0:T(8,128)S(1)}) custom-call(bf16[416,2048]{1,0:T(8,128)(2,1)} %grad_hbm.1, f32[416,2048]{1,0:T(8,128)} %momentum_hbm.1, bf16[2048,256]{1,0:T(8,128)(2,1)} %basis_hbm.1), custom_call_target="tpu_custom_call" | custom-call | tf_op jit(solution)/shard_map/pallas_call | solution.py:386
  60.9 2.7 %shard_map.59 = (f32[416,2048]{1,0:T(8,128)}, bf16[416,2048]{1,0:T(8,128)(2,1)}, bf16[2048,256]{1,0:T(8,128)(2,1)}) custom-call(f32[416,2048]{1,0:T(8,128)S(1)} %get-tuple-element.8.momentum, bf16[2048,256]{1,0:T(8,128)(2,1)S(1)} %get-tuple-element.9.rounded, bf16[416,256]{1,0:T(8,128)(2,1)S(1)} %get-tuple-element.10.ortho, ...), custom_call_target="tpu_custom_call" | custom-call | tf_op jit(solution)/shard_map/pallas_call | solution.py:459
